TPU v7x, 32 devices: a whole 2x2x4 slice. The times are simulated.
32 devices in a mesh: dp: 4 (over x, core), seq: 8 (over z, y).
Axes of the slice: x: 2, y: 2, z: 4, core: 2. Of those that a mesh axis runs over, the one named last changes fastest.
Arguments:
- tokens: bfloat16 [16, 2048, 768], P('dp', 'seq'), may hold values from -6 to 6
- lengths: int32 [16], P('dp'), may hold values from 32 to 2048, as said below
- cotangent: bfloat16 [16, 2048, 768], P('dp', 'seq'), may hold values from -6 to 6
- norm_gain: bfloat16 [2, 768], P(None, 'dp'), may hold values from 0.25 to 1.75
- norm_bias: bfloat16 [2, 768], P(None, 'dp'), may hold values from -1.5 to 1.5
- in_weight: bfloat16 [3, 4, 192, 192], P(None, None, 'dp'), may hold values from -0.4375 to 0.4375
- conv_taps: bfloat16 [3, 3, 768], P(None, None, 'dp'), may hold values from -3 to 3
- filter_in: bfloat16 [5, 128], P(None, 'dp'), may hold values from -2.5 to 2.5
- filter_mid: bfloat16 [128, 128], P('dp'), may hold values from -0.5 to 0.5
- filter_bias: bfloat16 [2, 128], P(None, 'dp'), may hold values from -1.5 to 1.5
- filter_out: bfloat16 [128, 768], P('dp', 'seq'), may hold values from -0.0234375 to 0.0234375
- out_weight: bfloat16 [4, 192, 192], P(None, 'dp'), may hold values from -0.4375 to 0.4375
- up_weight: bfloat16 [2, 4, 192, 768], P(None, None, 'dp'), may hold values from -0.4375 to 0.4375
- down_weight: bfloat16 [4, 768, 192], P(None, 'dp'), may hold values from -0.21875 to 0.21875
Outputs:
- out_tokens: bfloat16 [16, 2048, 768], P('dp', 'seq')
- grad_tokens: float32 [16, 2048, 768], P('dp', 'seq')
- grad_norm_gain: float32 [2, 768], P(None, 'dp')
- grad_norm_bias: float32 [2, 768], P(None, 'dp')
- grad_in_weight: float32 [3, 4, 192, 192], P(None, None, 'dp')
- grad_conv_taps: float32 [3, 3, 768], P(None, None, 'dp')
- grad_filter_in: float32 [5, 128], P(None, 'dp')
- grad_filter_mid: float32 [128, 128], P('dp')
- grad_filter_bias: float32 [2, 128], P(None, 'dp')
- grad_filter_out: float32 [128, 768], P('dp', 'seq')
- grad_out_weight: float32 [4, 192, 192], P(None, 'dp')
- grad_up_weight: float32 [2, 4, 192, 768], P(None, None, 'dp')
- grad_down_weight: float32 [4, 768, 192], P(None, 'dp')
Inputs may be any that keep to these rules, and one draw needn't show every extreme that they name: Each aligned block of 4 rows (the sequences of one index of dp) holds exactly one sequence of length 2048; the other lengths are shorter and have a heavy tail.
All inputs are finite; a program needn't handle non-finite values.
Results may differ from a plain program's by a relative error of at most 0.024.
Values may be sent and summed in bfloat16 or wider, within the bound.
No kernel may reach another device: no remote copies, remote signals or barrier semaphores. Data moves between devices by JAX's collectives and lax.ppermute only.
A program may use at most 192 MiB of HBM per device.

v0:
```python
import math

import jax
import jax.numpy as jnp
from jax import lax
from jax.sharding import PartitionSpec as P

GRID = 64
MB = 4


HIGH = lax.Precision.HIGHEST
EPS = 1e-05
SINE_FREQ = 10.0


def with_halo(value, sides, width):
    for axis, dim in sides:
        size, length = (lax.axis_size(axis), value.shape[dim])
        up = [(i, (i + 1) % size) for i in range(size - 1)]
        down = [(j, i) for i, j in up]
        last = lax.slice_in_dim(value, length - width, length, axis=dim)
        leading = lax.slice_in_dim(value, 0, width, axis=dim)
        before = lax.ppermute(last, axis, up)
        after = lax.ppermute(leading, axis, down)
        value = jnp.concatenate([before, value, after], axis=dim)
    return value


def as_sent(value):
    return jax.tree.map(lambda a: a.astype(jnp.bfloat16) if a.dtype == jnp.float32 else a, value)


def layer_norm(values, scales, offsets):
    average = jnp.mean(values, axis=-1, keepdims=True)
    centred = values - average
    variance = jnp.mean(centred * centred, axis=-1, keepdims=True)
    return centred * lax.rsqrt(variance + EPS) * scales + offsets


def gelu_gate(gate_up):
    return jax.nn.gelu(gate_up[0], approximate=False) * gate_up[1]


def lag_features(seq_length, size_fft):
    lags = jnp.arange(size_fft, dtype=jnp.int32)
    signed = jnp.where(lags < seq_length, lags, lags - size_fft)
    scaled = signed.astype(jnp.float32) / float(seq_length)
    feats = jnp.stack(
        [
            scaled,
            jnp.cos(math.pi * scaled),
            jnp.sin(math.pi * scaled),
            jnp.cos(2.0 * math.pi * scaled),
            jnp.sin(2.0 * math.pi * scaled),
        ],
        axis=1,
    )
    return (feats, jnp.abs(scaled))


def decay_rates(channel_ids, width):
    fast = math.log(100.0) / 0.3
    slow = math.log(100.0) / 1.5
    return slow + (fast - slow) * channel_ids.astype(jnp.float32) / float(width - 1)


def filter_values(feats, distance, rates, filter_in, filter_mid, filter_bias, filter_out):
    first = jnp.sin(SINE_FREQ * (jnp.dot(feats, filter_in, precision=HIGH) + filter_bias[0]))
    second = jnp.sin(SINE_FREQ * (jnp.dot(first, filter_mid, precision=HIGH) + filter_bias[1]))
    raw = jnp.dot(second, filter_out, precision=HIGH)
    return (raw * jnp.exp(-distance[:, None] * rates[None, :])).T


def tables(length):
    positions = jnp.arange(length, dtype=jnp.int32)
    angles = (positions[:, None] * positions[None, :] % length).astype(jnp.float32) * (
        2.0 * math.pi / length
    )
    return (jnp.cos(angles), jnp.sin(angles))


def twiddles(grid_rows, columns):
    product = (
        jnp.arange(grid_rows, dtype=jnp.int32)[:, None]
        * jnp.arange(columns, dtype=jnp.int32)[None, :]
    )
    angles = (product % (grid_rows * columns)).astype(jnp.float32) * (
        2.0 * math.pi / (grid_rows * columns)
    )
    return (jnp.cos(angles), jnp.sin(angles))


def right_mul(values, table):
    return jnp.einsum("...kc,cj->...kj", values, table, precision=HIGH)


def left_mul(table, values):
    return jnp.einsum("ka,...ac->...kc", table, values, precision=HIGH)


def spectrum(signal, grid_rows):
    data_rows = signal.shape[-2]
    columns = signal.shape[-1]
    row_cos, row_sin = tables(grid_rows)
    col_cos, col_sin = tables(columns)
    turn_cos, turn_sin = twiddles(grid_rows, columns)
    part_re = left_mul(row_cos[:, :data_rows], signal)
    part_im = -left_mul(row_sin[:, :data_rows], signal)
    turned_re = part_re * turn_cos + part_im * turn_sin
    turned_im = part_im * turn_cos - part_re * turn_sin
    spec_re = right_mul(turned_re, col_cos) + right_mul(turned_im, col_sin)
    spec_im = right_mul(turned_im, col_cos) - right_mul(turned_re, col_sin)
    return (spec_re, spec_im)


def inverse(spec_re, spec_im, data_rows):
    grid_rows = spec_re.shape[-2]
    columns = spec_re.shape[-1]
    row_cos, row_sin = tables(grid_rows)
    col_cos, col_sin = tables(columns)
    turn_cos, turn_sin = twiddles(grid_rows, columns)
    back_re = right_mul(spec_re, col_cos) - right_mul(spec_im, col_sin)
    back_im = right_mul(spec_re, col_sin) + right_mul(spec_im, col_cos)
    rotated_re = back_re * turn_cos - back_im * turn_sin
    rotated_im = back_re * turn_sin + back_im * turn_cos
    result = left_mul(row_cos[:data_rows], rotated_re) - left_mul(row_sin[:data_rows], rotated_im)
    return result / float(grid_rows * columns)


def long_conv(values, kernel):
    columns = kernel.shape[1] // GRID
    data_rows = values.shape[2] // columns
    shape_in = values.shape
    sig_re, sig_im = spectrum(values.reshape(shape_in[0], shape_in[1], data_rows, columns), GRID)
    ker_re, ker_im = spectrum(kernel.reshape(kernel.shape[0], 1, GRID, columns), GRID)
    prod_re = sig_re * ker_re - sig_im * ker_im
    prod_im = sig_re * ker_im + sig_im * ker_re
    return inverse(prod_re, prod_im, data_rows).reshape(shape_in)


def project(inputs, weights):
    blocked = inputs.reshape(inputs.shape[0], weights.shape[0], -1)
    return jnp.einsum("rnb,nbo->rno", blocked, weights, preferred_element_type=jnp.float32).reshape(
        inputs.shape[0], -1
    )


def project_back(gradients, weights):
    blocked = gradients.reshape(gradients.shape[0], weights.shape[0], -1)
    return jnp.einsum("rno,nbo->rnb", blocked, weights, preferred_element_type=jnp.float32).reshape(
        gradients.shape[0], -1
    )


def weight_grad(inputs, gradients, blocks):
    return jnp.einsum(
        "rnb,rno->nbo",
        inputs.reshape(inputs.shape[0], blocks, -1),
        gradients.reshape(gradients.shape[0], blocks, -1),
        preferred_element_type=jnp.float32,
    )


def tap_at(taps, which):
    return taps[which][:, None, None, :]


def per_device(
    tokens,
    lengths,
    cotangent,
    norm_gain,
    norm_bias,
    in_weight,
    conv_taps,
    filter_in,
    filter_mid,
    filter_bias,
    filter_out,
    out_weight,
    up_weight,
    down_weight,
):
    seq_local = tokens.shape[1]
    features = tokens.shape[2]
    per_batch = tokens.shape[0] // MB
    data_size = lax.axis_size("dp")
    seq_size = lax.axis_size("seq")
    seq_total = seq_local * seq_size
    places = lax.axis_index("seq") * seq_local + jnp.arange(seq_local, dtype=jnp.int32)
    chan_local = features // seq_size
    chan_ids = lax.axis_index("seq") * chan_local + jnp.arange(chan_local, dtype=jnp.int32)
    rates = decay_rates(chan_ids, features)
    feats, distance = lag_features(seq_total, 2 * seq_total)

    def collect():
        return (
            lax.all_gather(norm_gain, "dp", axis=1, tiled=True),
            lax.all_gather(norm_bias, "dp", axis=1, tiled=True),
            lax.all_gather(in_weight, "dp", axis=2, tiled=True),
            lax.all_gather(conv_taps, "dp", axis=2, tiled=True),
            lax.all_gather(filter_in, "dp", axis=1, tiled=True),
            lax.all_gather(filter_mid, "dp", axis=0, tiled=True),
            lax.all_gather(filter_bias, "dp", axis=1, tiled=True),
            lax.all_gather(filter_out, "dp", axis=0, tiled=True),
            lax.all_gather(out_weight, "dp", axis=1, tiled=True),
            lax.all_gather(up_weight, "dp", axis=2, tiled=True),
            lax.all_gather(down_weight, "dp", axis=1, tiled=True),
        )

    def make_kernel(first_w, mid_w, bias_w, out_w):
        return filter_values(feats, distance, rates, first_w, mid_w, bias_w, out_w)

    def micro_step(running, micro):
        inputs, counts, incoming = micro
        (
            gains_full,
            offsets_full,
            inner_full,
            taps_full,
            fin_full,
            fmid_full,
            fbias_full,
            fout_full,
            outer_full,
            upper_full,
            lower_full,
        ) = collect()
        gains_f = gains_full.astype(jnp.float32)
        offsets_f = offsets_full.astype(jnp.float32)
        taps_f = taps_full.astype(jnp.float32)
        blocks = inner_full.shape[1]
        batch_size = inputs.shape[0]
        row_count = batch_size * seq_local
        keep_mask = (places[None, :] < counts[:, None]).astype(jnp.float32)
        rows_in = inputs.astype(jnp.float32).reshape(row_count, features)
        kernel_ch, filter_pull = jax.vjp(
            make_kernel,
            fin_full.astype(jnp.float32),
            fmid_full.astype(jnp.float32),
            fbias_full.astype(jnp.float32),
            fout_full.astype(jnp.float32),
        )
        normed, norm_pull = jax.vjp(layer_norm, rows_in, gains_f[0], offsets_f[0])
        normed_low = normed.astype(jnp.bfloat16)
        streams = jnp.einsum(
            "rnb,snbo->srno",
            normed_low.reshape(row_count, blocks, -1),
            inner_full,
            preferred_element_type=jnp.float32,
        ).reshape(3, batch_size, seq_local, features)
        masked = streams * keep_mask[None, :, :, None]
        padded = with_halo(masked, (("seq", 2),), 1)
        short_out = (
            tap_at(taps_f, 0) * padded[:, :, 0:seq_local]
            + tap_at(taps_f, 1) * padded[:, :, 1 : seq_local + 1]
            + tap_at(taps_f, 2) * padded[:, :, 2:]
        )
        values = short_out[2] * short_out[0] * keep_mask[:, :, None]
        channels = lax.all_to_all(
            jnp.transpose(values, (2, 0, 1)).astype(jnp.bfloat16),
            "seq",
            split_axis=0,
            concat_axis=2,
            tiled=True,
        ).astype(jnp.float32)
        conv_ch, conv_pull = jax.vjp(long_conv, channels, kernel_ch)
        conv_tok = jnp.transpose(
            lax.all_to_all(as_sent(conv_ch), "seq", split_axis=2, concat_axis=0, tiled=True).astype(
                conv_ch.dtype
            ),
            (1, 2, 0),
        )
        gated_in = (conv_tok * short_out[1]).reshape(row_count, features).astype(jnp.bfloat16)
        middle = rows_in + project(gated_in, outer_full)
        normed_two, norm_pull_two = jax.vjp(layer_norm, middle, gains_f[1], offsets_f[1])
        normed_two_low = normed_two.astype(jnp.bfloat16)
        gate_up = jnp.einsum(
            "rnb,snbo->srno",
            normed_two_low.reshape(row_count, blocks, -1),
            upper_full,
            preferred_element_type=jnp.float32,
        ).reshape(2, row_count, -1)
        hidden, gate_pull = jax.vjp(gelu_gate, gate_up)
        hidden_low = hidden.astype(jnp.bfloat16)
        result = middle + project(hidden_low, lower_full)
        output = result.astype(jnp.bfloat16).reshape(batch_size, seq_local, features)
        grad_out = incoming.reshape(row_count, features)
        grad_lower = weight_grad(hidden_low, grad_out, blocks)
        (grad_pair,) = gate_pull(project_back(grad_out, lower_full))
        grad_pair_low = grad_pair.astype(jnp.bfloat16).reshape(2, row_count, blocks, -1)
        grad_upper = jnp.einsum(
            "rnb,srno->snbo",
            normed_two_low.reshape(row_count, blocks, -1),
            grad_pair_low,
            preferred_element_type=jnp.float32,
        )
        grad_normed_two = jnp.einsum(
            "srno,snbo->rnb", grad_pair_low, upper_full, preferred_element_type=jnp.float32
        ).reshape(row_count, features)
        grad_middle_norm, grad_gain_two, grad_offset_two = norm_pull_two(grad_normed_two)
        grad_middle = grad_out.astype(jnp.float32) + grad_middle_norm
        grad_branch = grad_middle.astype(jnp.bfloat16)
        grad_outer = weight_grad(gated_in, grad_branch, blocks)
        grad_gated = project_back(grad_branch, outer_full).reshape(batch_size, seq_local, features)
        grad_conv = grad_gated * short_out[1]
        grad_short_one = grad_gated * conv_tok
        grad_channels = lax.all_to_all(
            jnp.transpose(grad_conv, (2, 0, 1)).astype(jnp.bfloat16),
            "seq",
            split_axis=0,
            concat_axis=2,
            tiled=True,
        ).astype(jnp.float32)
        grad_values_ch, grad_kernel = conv_pull(grad_channels)
        grad_fin, grad_fmid, grad_fbias, grad_fout = filter_pull(grad_kernel)
        grad_values = (
            jnp.transpose(
                lax.all_to_all(
                    as_sent(grad_values_ch), "seq", split_axis=2, concat_axis=0, tiled=True
                ).astype(grad_values_ch.dtype),
                (1, 2, 0),
            )
            * keep_mask[:, :, None]
        )
        grad_short = jnp.stack(
            [grad_values * short_out[2], grad_short_one, grad_values * short_out[0]]
        )
        grad_padded = with_halo(as_sent(grad_short), (("seq", 2),), 1).astype(grad_short.dtype)
        grad_taps = jnp.stack(
            [
                jnp.sum(grad_short * padded[:, :, 0:seq_local], axis=(1, 2)),
                jnp.sum(grad_short * padded[:, :, 1 : seq_local + 1], axis=(1, 2)),
                jnp.sum(grad_short * padded[:, :, 2:], axis=(1, 2)),
            ]
        )
        grad_masked = (
            tap_at(taps_f, 0) * grad_padded[:, :, 2:]
            + tap_at(taps_f, 1) * grad_padded[:, :, 1 : seq_local + 1]
            + tap_at(taps_f, 2) * grad_padded[:, :, 0:seq_local]
        )
        grad_streams = (
            (grad_masked * keep_mask[None, :, :, None])
            .astype(jnp.bfloat16)
            .reshape(3, row_count, blocks, -1)
        )
        grad_inner = jnp.einsum(
            "rnb,srno->snbo",
            normed_low.reshape(row_count, blocks, -1),
            grad_streams,
            preferred_element_type=jnp.float32,
        )
        grad_normed = jnp.einsum(
            "srno,snbo->rnb", grad_streams, inner_full, preferred_element_type=jnp.float32
        ).reshape(row_count, features)
        grad_rows, grad_gain_one, grad_offset_one = norm_pull(grad_normed)
        grad_inputs = (grad_middle + grad_rows).reshape(batch_size, seq_local, features)
        pieces = (
            jnp.stack([grad_gain_one, grad_gain_two]),
            jnp.stack([grad_offset_one, grad_offset_two]),
            grad_inner,
            grad_taps,
            grad_fin,
            grad_fmid,
            grad_fbias,
            grad_fout,
            grad_outer,
            grad_upper,
            grad_lower,
        )
        updated = tuple((total + piece for total, piece in zip(running, pieces)))
        return (updated, (output, grad_inputs))

    initial = (
        jnp.zeros((2, features), jnp.float32),
        jnp.zeros((2, features), jnp.float32),
        jnp.zeros(
            (3, in_weight.shape[1], in_weight.shape[2] * data_size, in_weight.shape[3]), jnp.float32
        ),
        jnp.zeros((3, 3, features), jnp.float32),
        jnp.zeros((filter_in.shape[0], filter_in.shape[1] * data_size), jnp.float32),
        jnp.zeros((filter_mid.shape[0] * data_size, filter_mid.shape[1]), jnp.float32),
        jnp.zeros((2, filter_bias.shape[1] * data_size), jnp.float32),
        jnp.zeros((filter_out.shape[0] * data_size, filter_out.shape[1]), jnp.float32),
        jnp.zeros(
            (out_weight.shape[0], out_weight.shape[1] * data_size, out_weight.shape[2]), jnp.float32
        ),
        jnp.zeros(
            (2, up_weight.shape[1], up_weight.shape[2] * data_size, up_weight.shape[3]), jnp.float32
        ),
        jnp.zeros(
            (down_weight.shape[0], down_weight.shape[1] * data_size, down_weight.shape[2]),
            jnp.float32,
        ),
    )
    micro_inputs = (
        tokens.reshape(MB, per_batch, seq_local, features),
        lengths.reshape(MB, per_batch),
        cotangent.reshape(MB, per_batch, seq_local, features),
    )
    totals, (outputs, grad_tokens) = lax.scan(micro_step, initial, micro_inputs)
    outputs = outputs.reshape(tokens.shape)
    grad_tokens = grad_tokens.reshape(tokens.shape)
    summed = (
        lax.psum(totals[0].astype(jnp.bfloat16), "seq").astype(jnp.float32),
        lax.psum(totals[1].astype(jnp.bfloat16), "seq").astype(jnp.float32),
        lax.psum(totals[2].astype(jnp.bfloat16), "seq").astype(jnp.float32),
        lax.psum(totals[3].astype(jnp.bfloat16), "seq").astype(jnp.float32),
        lax.psum(totals[4].astype(jnp.bfloat16), "seq").astype(jnp.float32),
        lax.psum(totals[5].astype(jnp.bfloat16), "seq").astype(jnp.float32),
        lax.psum(totals[6].astype(jnp.bfloat16), "seq").astype(jnp.float32),
        lax.psum(totals[8].astype(jnp.bfloat16), "seq").astype(jnp.float32),
        lax.psum(totals[9].astype(jnp.bfloat16), "seq").astype(jnp.float32),
        lax.psum(totals[10].astype(jnp.bfloat16), "seq").astype(jnp.float32),
    )
    shares = (
        lax.psum_scatter(
            summed[0].astype(jnp.bfloat16), "dp", scatter_dimension=1, tiled=True
        ).astype(jnp.float32),
        lax.psum_scatter(
            summed[1].astype(jnp.bfloat16), "dp", scatter_dimension=1, tiled=True
        ).astype(jnp.float32),
        lax.psum_scatter(
            summed[2].astype(jnp.bfloat16), "dp", scatter_dimension=2, tiled=True
        ).astype(jnp.float32),
        lax.psum_scatter(
            summed[3].astype(jnp.bfloat16), "dp", scatter_dimension=2, tiled=True
        ).astype(jnp.float32),
        lax.psum_scatter(
            summed[4].astype(jnp.bfloat16), "dp", scatter_dimension=1, tiled=True
        ).astype(jnp.float32),
        lax.psum_scatter(
            summed[5].astype(jnp.bfloat16), "dp", scatter_dimension=0, tiled=True
        ).astype(jnp.float32),
        lax.psum_scatter(
            summed[6].astype(jnp.bfloat16), "dp", scatter_dimension=1, tiled=True
        ).astype(jnp.float32),
        lax.psum_scatter(
            totals[7].astype(jnp.bfloat16), "dp", scatter_dimension=0, tiled=True
        ).astype(jnp.float32),
        lax.psum_scatter(
            summed[7].astype(jnp.bfloat16), "dp", scatter_dimension=1, tiled=True
        ).astype(jnp.float32),
        lax.psum_scatter(
            summed[8].astype(jnp.bfloat16), "dp", scatter_dimension=2, tiled=True
        ).astype(jnp.float32),
        lax.psum_scatter(
            summed[9].astype(jnp.bfloat16), "dp", scatter_dimension=1, tiled=True
        ).astype(jnp.float32),
    )
    return (
        outputs,
        grad_tokens,
        shares[0],
        shares[1],
        shares[2],
        shares[3],
        shares[4],
        shares[5],
        shares[6],
        shares[7],
        shares[8],
        shares[9],
        shares[10],
    )


def solution(mesh):
    placed = (
        P("dp", "seq", None),
        P("dp"),
        P("dp", "seq", None),
        P(None, "dp"),
        P(None, "dp"),
        P(None, None, "dp", None),
        P(None, None, "dp"),
        P(None, "dp"),
        P("dp", None),
        P(None, "dp"),
        P("dp", "seq"),
        P(None, "dp", None),
        P(None, None, "dp", None),
        P(None, "dp", None),
    )
    return jax.shard_map(
        per_device,
        mesh=mesh,
        in_specs=placed,
        out_specs=(
            P("dp", "seq", None),
            P("dp", "seq", None),
            P(None, "dp"),
            P(None, "dp"),
            P(None, None, "dp", None),
            P(None, None, "dp"),
            P(None, "dp"),
            P("dp", None),
            P(None, "dp"),
            P("dp", "seq"),
            P(None, "dp", None),
            P(None, None, "dp", None),
            P(None, "dp", None),
        ),
        check_vma=False,
    )
```

profile of v0, /device:TPU:0, one launch (start us, length us, event | category | flops | bytes accessed | tf_op | source)
XLA Modules:
  0.0 2438.3 jit_solution(16944667079485798893)
XLA Ops:
  18.4 2038.4 %while.39 = (s32[]{:T(128)}, f32[2,768]{1,0:T(2,128)}, f32[2,768]{1,0:T(2,128)}, f32[3,4,192,192]{2,3,0,1:T(8,128)}, f32[3,3,768]{2,1,0:T(4,128)}, /*index=5*/f3...) while((s32[]{:T(128)}, f32[2,768]{1,0:T(2,128)}, ...), condition=%wide.region_18.19_spmd.clone.clone, body=%wide.region_0.18_spmd.clone.clone.sunk | while | flops 17785057280 | bytes 737910208 | solution.py:402
  35.9 13.0 all_gather.102
  231.1 13.4 reduce.54
  415.6 12.6 reduce.56
  542.8 11.8 all_gather.102
  736.8 13.4 reduce.54
  923.4 12.6 reduce.56
  1245.2 13.4 reduce.54
  1431.8 12.6 reduce.56
  1754.0 13.4 reduce.54
  1940.6 12.6 reduce.56
  2079.2 11.9 reduce-scatter.46.cloned.1.call-done
  2093.4 21.5 reduce-scatter.30.cloned.1.call-done
  2114.9 28.3 %reduce-scatter.26.cloned.1.call-done = bf16[3,4,48,192]{3,2,1,0:T(8,128)(2,1)} async-done(((bf16[3,4,192,192]{3,2,1,0:T(8,128)(2,1)}), bf16[3,4,48,192]{3,2,1,0:T(8,128)(2,1)}) %reduce-scatter.26.cloned.1.call-update) | async-done | bytes 221200 | tf_op jit(solution)/shard_map/reduce_scatter | solution.py:424
  2143.2 35.6 %reduce-scatter.32.cloned.1.call-done = bf16[2,4,48,768]{3,2,1,0:T(8,128)(2,1)} async-done(((bf16[2,4,192,768]{3,2,1,0:T(8,128)(2,1)}), bf16[2,4,48,768]{3,2,1,0:T(8,128)(2,1)}) %reduce-scatter.32.cloned.1.call-update) | async-done | bytes 589840 | tf_op jit(solution)/shard_map/reduce_scatter | solution.py:445
  2178.8 21.9 reduce-scatter.44.cloned.1.call-done
  2201.5 21.0 reduce-scatter.42.cloned.1.call-done
  2223.3 21.5 reduce-scatter.38.cloned.1.call-done
  2245.6 21.9 reduce-scatter.36.cloned.1.call-done
  2268.4 21.3 reduce-scatter.40.cloned.1.call-done
  2290.8 20.9 reduce-scatter.34.cloned.1.call-done
  2313.1 20.1 reduce-scatter.28.cloned.1.call-done
  2333.3 38.2 %all-reduce.4 = (bf16[2,192]{1,0:T(2,128)(2,1)S(1)}, bf16[2,192]{1,0:T(2,128)(2,1)S(1)}, bf16[3,3,192]{2,1,0:T(4,128)(2,1)S(1)}, bf16[5,32]{1,0:T(8,128)(2,1)S(1...) all-reduce(bf16[2,192]{1,0:T(2,128)(2,1)S(1)} %copy.620, ...), channel_id=1, replica_groups=mesh['dp'=4,'seq'=8] {'seq'}, use_global_device_ids=true, to_apply=%region_19.20 | all-reduce | flops 6816 | bytes 27264 | tf_op jit(solution)/shard_map/psum | solution.py:406
  2375.0 48.9 %all-reduce.8.cloned.1.call-done = (bf16[4,192,192]{1,2,0:T(8,128)(2,1)}, bf16[3,4,48,192]{3,2,1,0:T(8,128)(2,1)}, bf16[4,48,192]{2,1,0:T(8,128)(2,1)}, bf16[2,4,48,768]{3,2,1,0:T(8,128)(2,1)}) async-done(((bf16[4,192,192]{1,2,0:T(8,128)(2,1)}, bf16[3,4,48,192]{3,2,1,0:T(8,128)(2,1)}, bf16[4,48,192]{2,1,0:T(8,128)(2,1)}, bf16[2,4,48,768]{3,2,1,0:T(8,128)(2,1)}), (bf16[4,192,192]{1,2,0:T(8,128)(2,1)}, ...) | async-done | bytes 1179664 | tf_op jit(solution)/shard_map/psum | solution.py:415
  (1898 shorter events, 1948.5 us)
Async XLA Ops:
  18.4 259.3 %all-gather.19.cloned.1.call-start = ((), (), s32[]{:S(2)}) async-start(), calls=%async_computation.27 | async-start | bytes 1966080 | tf_op jit(solution)/shard_map/while/body/eval_jaxpr/all_gather | solution.py:209
  19.1 265.9 %all-gather.21.cloned.1.call-start = ((), (), s32[]{:S(2)}) async-start(), calls=%async_computation.28 | async-start | bytes 2949120 | tf_op jit(solution)/shard_map/while/body/eval_jaxpr/all_gather | solution.py:208
  57.2 67.2 %collective-permute-start.1 = (f32[3,1,1,768]{3,2,1,0:T(1,128)}, f32[3,1,1,768]{3,2,1,0:T(1,128)}, u32[]{:S(2)}, u32[]{:S(2)}) collective-permute-start(f32[3,1,1,768]{3,2,1,0:T(1,128)} %copy.861), channel_id=1, source_target_pairs={{0,1},{1,2},{2,3},{3,4},{4,5},{5,6},{6,7},{8,9},{9,10},{10,11},{11... | collective-permute-start | bytes 27656 | tf_op jit(solution)/shard_map/while/body/eval_jaxpr/ppermute | solution.py:24
  526.5 256.8 %all-gather.19.cloned.1.call-start = ((), (), s32[]{:S(2)}) async-start(), calls=%async_computation.27 | async-start | bytes 1966080 | tf_op jit(solution)/shard_map/while/body/eval_jaxpr/all_gather | solution.py:209
  527.2 263.4 %all-gather.21.cloned.1.call-start = ((), (), s32[]{:S(2)}) async-start(), calls=%async_computation.28 | async-start | bytes 2949120 | tf_op jit(solution)/shard_map/while/body/eval_jaxpr/all_gather | solution.py:208
  562.8 67.2 %collective-permute-start.1 = (f32[3,1,1,768]{3,2,1,0:T(1,128)}, f32[3,1,1,768]{3,2,1,0:T(1,128)}, u32[]{:S(2)}, u32[]{:S(2)}) collective-permute-start(f32[3,1,1,768]{3,2,1,0:T(1,128)} %copy.861), channel_id=1, source_target_pairs={{0,1},{1,2},{2,3},{3,4},{4,5},{5,6},{6,7},{8,9},{9,10},{10,11},{11... | collective-permute-start | bytes 27656 | tf_op jit(solution)/shard_map/while/body/eval_jaxpr/ppermute | solution.py:24
  567.8 61.2 %collective-permute-start = (f32[3,1,1,768]{3,2,1,0:T(1,128)}, f32[3,1,1,768]{3,2,1,0:T(1,128)}, u32[]{:S(2)}, u32[]{:S(2)}) collective-permute-start(f32[3,1,1,768]{3,2,1,0:T(1,128)} %copy.857), channel_id=1, source_target_pairs={{1,0},{2,1},{3,2},{4,3},{5,4},{6,5},{7,6},{9,8},{10,9},{11,10},{12... | collective-permute-start | bytes 27656 | tf_op jit(solution)/shard_map/while/body/eval_jaxpr/ppermute | solution.py:25
  1035.2 256.6 %all-gather.19.cloned.1.call-start = ((), (), s32[]{:S(2)}) async-start(), calls=%async_computation.27 | async-start | bytes 1966080 | tf_op jit(solution)/shard_map/while/body/eval_jaxpr/all_gather | solution.py:209
  1035.8 263.3 %all-gather.21.cloned.1.call-start = ((), (), s32[]{:S(2)}) async-start(), calls=%async_computation.28 | async-start | bytes 2949120 | tf_op jit(solution)/shard_map/while/body/eval_jaxpr/all_gather | solution.py:208
  1071.3 67.2 %collective-permute-start.1 = (f32[3,1,1,768]{3,2,1,0:T(1,128)}, f32[3,1,1,768]{3,2,1,0:T(1,128)}, u32[]{:S(2)}, u32[]{:S(2)}) collective-permute-start(f32[3,1,1,768]{3,2,1,0:T(1,128)} %copy.861), channel_id=1, source_target_pairs={{0,1},{1,2},{2,3},{3,4},{4,5},{5,6},{6,7},{8,9},{9,10},{10,11},{11... | collective-permute-start | bytes 27656 | tf_op jit(solution)/shard_map/while/body/eval_jaxpr/ppermute | solution.py:24
  1076.2 61.2 %collective-permute-start = (f32[3,1,1,768]{3,2,1,0:T(1,128)}, f32[3,1,1,768]{3,2,1,0:T(1,128)}, u32[]{:S(2)}, u32[]{:S(2)}) collective-permute-start(f32[3,1,1,768]{3,2,1,0:T(1,128)} %copy.857), channel_id=1, source_target_pairs={{1,0},{2,1},{3,2},{4,3},{5,4},{6,5},{7,6},{9,8},{10,9},{11,10},{12... | collective-permute-start | bytes 27656 | tf_op jit(solution)/shard_map/while/body/eval_jaxpr/ppermute | solution.py:25
  1543.6 256.9 %all-gather.19.cloned.1.call-start = ((), (), s32[]{:S(2)}) async-start(), calls=%async_computation.27 | async-start | bytes 1966080 | tf_op jit(solution)/shard_map/while/body/eval_jaxpr/all_gather | solution.py:209
  1544.4 263.4 %all-gather.21.cloned.1.call-start = ((), (), s32[]{:S(2)}) async-start(), calls=%async_computation.28 | async-start | bytes 2949120 | tf_op jit(solution)/shard_map/while/body/eval_jaxpr/all_gather | solution.py:208
  1580.0 67.2 %collective-permute-start.1 = (f32[3,1,1,768]{3,2,1,0:T(1,128)}, f32[3,1,1,768]{3,2,1,0:T(1,128)}, u32[]{:S(2)}, u32[]{:S(2)}) collective-permute-start(f32[3,1,1,768]{3,2,1,0:T(1,128)} %copy.861), channel_id=1, source_target_pairs={{0,1},{1,2},{2,3},{3,4},{4,5},{5,6},{6,7},{8,9},{9,10},{10,11},{11... | collective-permute-start | bytes 27656 | tf_op jit(solution)/shard_map/while/body/eval_jaxpr/ppermute | solution.py:24
  2065.9 77.3 %reduce-scatter.26.cloned.1.call-start = ((), (), s32[]{:S(2)}) async-start(), calls=%async_computation.15 | async-start | bytes 1474560 | tf_op jit(solution)/shard_map/reduce_scatter | solution.py:424
  2067.6 111.2 %reduce-scatter.32.cloned.1.call-start = ((), (), s32[]{:S(2)}) async-start(), calls=%async_computation.18 | async-start | bytes 2949120 | tf_op jit(solution)/shard_map/reduce_scatter | solution.py:445
  2071.8 128.9 %reduce-scatter.44.cloned.1.call-start = ((), (), s32[]{:S(2)}) async-start(), calls=%async_computation.24 | async-start | bytes 40960
  2073.1 149.3 %reduce-scatter.42.cloned.1.call-start = ((), (), s32[]{:S(2)}) async-start(), calls=%async_computation.23 | async-start | bytes 40960
  2074.0 170.8 %reduce-scatter.38.cloned.1.call-start = ((), (), s32[]{:S(2)}) async-start(), calls=%async_computation.21 | async-start | bytes 245760
  2074.9 192.6 %reduce-scatter.36.cloned.1.call-start = ((), (), s32[]{:S(2)}) async-start(), calls=%async_computation.20 | async-start | bytes 245760
  2075.8 213.9 %reduce-scatter.40.cloned.1.call-start = ((), (), s32[]{:S(2)}) async-start(), calls=%async_computation.22 | async-start | bytes 245760
  2077.6 234.0 %reduce-scatter.34.cloned.1.call-start = ((), (), s32[]{:S(2)}) async-start(), calls=%async_computation.19 | async-start | bytes 40960
  2078.4 254.8 %reduce-scatter.28.cloned.1.call-start = ((), (), s32[]{:S(2)}) async-start(), calls=%async_computation.16 | async-start | bytes 40960 | tf_op jit(solution)/shard_map/reduce_scatter | solution.py:433
  2079.1 344.8 %all-reduce.8.cloned.1.call-start = ((), (), s32[]{:S(2)}) async-start(), calls=%async_computation.26 | async-start | bytes 2752512 | tf_op jit(solution)/shard_map/psum | solution.py:415
  (515 other events, 3913.2 us)
Sparse Core Ops, SparseCore 0:
  20.8 24.2 all-gather.18
  63.5 25.6 all-gather.20
  528.9 20.7 all-gather.18
  569.2 25.5 all-gather.20
  1037.3 20.5 all-gather.18
  1077.6 25.5 all-gather.20
  1546.1 20.7 all-gather.18
  1586.4 25.5 all-gather.20
Sparse Core Ops, SparseCore 1:
  2065.1 25.9 reduce-scatter.45
  2094.1 20.7 reduce-scatter.29
  2117.5 25.6 reduce-scatter.25
  2145.7 33.0 reduce-scatter.31
  2181.3 19.3 reduce-scatter.43
  2203.1 19.3 reduce-scatter.41
  2224.9 19.7 reduce-scatter.37
  2247.7 19.7 reduce-scatter.35
  2270.0 19.7 reduce-scatter.39
  2292.3 19.3 reduce-scatter.33
  2313.9 19.3 reduce-scatter.27
  2338.2 85.6 all-reduce.7
where the time goes:
time: 2450 us; the launch traced here: 2440 us
  matrix products  775 us (32%)
  local copies, waits for them, and re-layouts  524 us (21%)
  other arithmetic  377 us (15%)
  waiting for transfers between devices  309 us (13%)
  blocking collectives  280 us (11%)
  starting transfers between devices  145 us (6%)
    dot_general x96, matrix products, right_mul(): return jnp.einsum('...kc,cj->...kj', values, table, precision=HIGH)  302 us
    while x1008, local copies, waits for them, and re-layouts  173 us
    dot_general x48, matrix products, left_mul(): return jnp.einsum('ka,...ac->...kc', table, values, precision=HIGH)  171 us
    unnamed x19, waiting for transfers between devices  141 us
    while x8, other arithmetic  104 us
    dot_general x12, matrix products, filter_values(): jnp.dot(first, filter_mid, precision=HIGH) + filter_bias[1]  89.5 us
    convert_element_type x16, local copies, waits for them, and re-layouts, as_sent(): a.astype(jnp.bfloat16)  69.9 us
    dot_general x12, matrix products, filter_values(): raw = jnp.dot(second, filter_out, precision=HIGH)  60.9 us
  transfers between devices with their start and end apart: 52, of which 16 were waited for; matrix products, arithmetic and copies ran while one was open for 39% of the time, Pallas kernels for 0%

commit v1 on v0

v1 whole, which is shorter than its diff:
```python
import functools
import math

import jax
import jax.numpy as jnp
import numpy as np
from jax import lax
from jax.experimental import pallas as pl
from jax.experimental.pallas import tpu as pltpu
from jax.sharding import PartitionSpec as P

F32 = jnp.float32
BF16 = jnp.bfloat16
EPS = 1e-05
SINE_FREQ = 10.0
GROUP = 3
COLS = 128
HALF_ROWS = 16
FULL_ROWS = 32
FREQ_ROWS = 17
STAT_ROWS = 16
VMEM = pltpu.CompilerParams(vmem_limit_bytes=56 * 1024 * 1024)


def stage_tables():
    k1 = np.arange(FREQ_ROWS)[:, None, None]
    t1 = np.arange(FULL_ROWS)[None, :, None]
    t2 = np.arange(COLS)[None, None, :]
    phase = 2.0 * np.pi * ((k1 * (t1 * COLS + t2)) % 4096) / 4096.0
    both = np.stack([np.cos(phase), -np.sin(phase)], axis=1)
    out = np.zeros((8, FREQ_ROWS, 2, 16, FULL_ROWS, 16), np.float32)
    for a in range(16):
        out[:, :, :, a, :, a] = np.moveaxis(both[..., a::16], -1, 0)
    first = out.reshape(8, FREQ_ROWS * 32, FULL_ROWS * 16)
    theta = 2.0 * np.pi * (np.outer(np.arange(COLS), np.arange(COLS)) % COLS) / COLS
    second = np.block([[np.cos(theta), np.sin(theta)], [-np.sin(theta), np.cos(theta)]])
    return first, second


def lag_table(seq_total):
    lags = np.arange(2 * seq_total)
    scaled = np.where(lags < seq_total, lags, lags - 2 * seq_total) / float(seq_total)
    feats = np.stack(
        [
            scaled,
            np.cos(np.pi * scaled),
            np.sin(np.pi * scaled),
            np.cos(2.0 * np.pi * scaled),
            np.sin(2.0 * np.pi * scaled),
        ],
        axis=1,
    ).astype(np.float32)
    parts, rest = [], feats
    for _ in range(3):
        piece = rest.astype(jnp.bfloat16)
        parts.append(piece.astype(np.float32))
        rest = rest - piece.astype(np.float32)
    table = np.zeros((2 * seq_total, 16), np.float32)
    table[:, :15] = np.concatenate(parts, axis=1)
    return table


def dot(a, b):
    return jnp.dot(a, b, preferred_element_type=F32)


def low_lanes(rows):
    return lax.broadcasted_iota(jnp.int32, (rows, 128), 1) < 64


def tiles(value):
    return [value[:, 128 * i : 128 * (i + 1)] for i in range(value.shape[1] // 128)]


def half_turn(value):
    return pltpu.roll(value, 64, axis=1)


def stacked(value):
    first, second, last = tiles(value)
    low = low_lanes(value.shape[0])
    zero = jnp.zeros_like(last)
    return jnp.concatenate(
        [
            jnp.concatenate([first, jnp.where(low, last, zero)], axis=1),
            jnp.concatenate([second, jnp.where(low, zero, last)], axis=1),
        ],
        axis=0,
    )


def packed(value):
    rows = value.shape[0] // 2
    low = low_lanes(rows)
    last = jnp.where(low, value[:rows, 128:], value[rows:, 128:])
    return jnp.concatenate([value[:rows, :128], value[rows:, :128], last], axis=1)


def pair_sum(value):
    first, second, last = tiles(value)
    low = low_lanes(value.shape[0])
    zero = jnp.zeros_like(last)
    return (
        jnp.sum(first + jnp.where(low, last, zero), axis=1, keepdims=True),
        jnp.sum(second + jnp.where(low, zero, last), axis=1, keepdims=True),
    )


def spread(col_a, col_b, rows):
    wide_a = jnp.broadcast_to(col_a, (rows, 128))
    wide_b = jnp.broadcast_to(col_b, (rows, 128))
    return jnp.concatenate([wide_a, wide_b, jnp.where(low_lanes(rows), wide_a, wide_b)], axis=1)


def to_rows(columns, rows):
    lane = lax.broadcasted_iota(jnp.int32, (rows, 128), 1)
    out = jnp.zeros((rows, 128), F32)
    for at, column in enumerate(columns):
        out = jnp.where(lane == at, jnp.broadcast_to(column, (rows, 128)), out)
    if rows % 128:
        out = jnp.concatenate([out, jnp.zeros((128 - rows, 128), F32)], axis=0)
    return out.T[:8, :rows]


def to_columns(values):
    rows = values.shape[1]
    if rows % 128:
        values = jnp.concatenate([values, jnp.zeros((8, 128 - rows), F32)], axis=1)
    tall = jnp.concatenate([values, jnp.zeros((120, values.shape[1]), F32)], axis=0)
    return tall.T[:rows]


def split_rows(values):
    high = values.astype(BF16).astype(F32)
    return jnp.concatenate([high, values - high], axis=0).astype(BF16)


def join_rows(values):
    wide = values.astype(F32)
    return wide[:8] + wide[8:]


def position_mask(start, rows, count_a, count_b):
    place = start + lax.broadcasted_iota(jnp.int32, (rows, 128), 0)
    keep_a = (place < count_a).astype(F32)
    keep_b = (place < count_b).astype(F32)
    return jnp.concatenate([keep_a, keep_b, jnp.where(low_lanes(rows), keep_a, keep_b)], axis=1)


def sine_pair(angle):
    turns = jnp.floor(angle * (1.0 / math.pi) + 0.5)
    rest = angle - turns * 3.140625
    rest = rest - turns * 9.675025939941406e-4
    rest = rest - turns * 1.5099579909783764e-7
    half = turns * 0.5
    sign = 1.0 - 4.0 * (half - jnp.floor(half))
    square = rest * rest
    sine = square * (-1.0 / 39916800.0) + 1.0 / 362880.0
    sine = sine * square - 1.0 / 5040.0
    sine = sine * square + 1.0 / 120.0
    sine = sine * square - 1.0 / 6.0
    sine = rest + rest * square * sine
    cosine = square * (1.0 / 479001600.0) - 1.0 / 3628800.0
    cosine = cosine * square + 1.0 / 40320.0
    cosine = cosine * square - 1.0 / 720.0
    cosine = cosine * square + 1.0 / 24.0
    cosine = cosine * square - 0.5
    cosine = 1.0 + square * cosine
    return sine * sign, cosine * sign


MILLS = (
    0.11962639,
    0.12079834,
    0.0996376,
    0.12946887,
    -0.05539326,
    0.20820602,
    -0.15827569,
    0.03593167,
)


def normal_parts(value):
    bell = jnp.exp(value * value * -0.5)
    base = 1.0 + 0.3 * jnp.abs(value)
    inv = pl.reciprocal(base, approx=True)
    inv = inv * (2.0 - base * inv)
    tail = inv * MILLS[7] + MILLS[6]
    for coefficient in MILLS[5::-1]:
        tail = tail * inv + coefficient
    tail = tail * inv * bell
    return jnp.where(value >= 0.0, 1.0 - tail, tail), bell * (1.0 / math.sqrt(2.0 * math.pi))


def pack_pair(a, b, block):
    rows = a.shape[0]
    low = low_lanes(rows)
    base = 3 * (block // 2)
    ta = [a[:, 128 * (base + i) : 128 * (base + i + 1)] for i in range(3)]
    tb = [b[:, 128 * (base + i) : 128 * (base + i + 1)] for i in range(3)]
    if block % 2 == 0:
        parts = [ta[0], tb[0], jnp.where(low, ta[1], half_turn(tb[1]))]
    else:
        parts = [
            jnp.where(low, half_turn(ta[1]), half_turn(ta[2])),
            jnp.where(low, half_turn(tb[1]), half_turn(tb[2])),
            jnp.where(low, half_turn(ta[2]), tb[2]),
        ]
    return jnp.concatenate(parts, axis=1)


def unpack_pairs(even, odd):
    low = low_lanes(even.shape[0])
    ea, eb, el = tiles(even)
    oa, ob, ol = tiles(odd)
    a = [ea, jnp.where(low, el, half_turn(oa)), jnp.where(low, half_turn(oa), half_turn(ol))]
    b = [eb, jnp.where(low, half_turn(el), half_turn(ob)), jnp.where(low, half_turn(ob), ol)]
    return jnp.concatenate(a, axis=1), jnp.concatenate(b, axis=1)


def row_stats(value):
    mean = jnp.mean(value, axis=1, keepdims=True)
    centred = value - mean
    variance = jnp.mean(centred * centred, axis=1, keepdims=True)
    return mean, lax.rsqrt(variance + EPS)


def pack_tokens_kernel(x_ref, out_ref):
    rows = x_ref.shape[1]
    a = x_ref[0].astype(F32)
    b = x_ref[1].astype(F32)
    stats = split_rows(to_rows(row_stats(a) + row_stats(b), rows))
    for block in range(4):
        out_ref[block, :rows, :] = pack_pair(a, b, block).astype(BF16)
        out_ref[block, rows:, :rows] = stats


def pack_tokens(tokens):
    count, rows, width = tokens.shape
    return pl.pallas_call(
        pack_tokens_kernel,
        grid=(count // 2,),
        in_specs=[pl.BlockSpec((2, rows, width), lambda i: (i, 0, 0))],
        out_specs=pl.BlockSpec((4, rows + STAT_ROWS, 384), lambda i: (i, 0, 0)),
        out_shape=jax.ShapeDtypeStruct((2 * count, rows + STAT_ROWS, 384), BF16),
        compiler_params=VMEM,
        name="pack_tokens",
    )(tokens)


def pack_cotangent_kernel(x_ref, after_ref, out_ref):
    a = x_ref[0].astype(F32)
    b = x_ref[1].astype(F32)
    for block in range(4):
        out_ref[block] = pack_pair(a, b, block).astype(BF16)


def pack_cotangent(cotangent, after):
    count, rows, width = cotangent.shape
    return pl.pallas_call(
        pack_cotangent_kernel,
        grid=(count // 2,),
        in_specs=[
            pl.BlockSpec((2, rows, width), lambda i: (i, 0, 0)),
            pl.BlockSpec(memory_space=pl.ANY),
        ],
        out_specs=pl.BlockSpec((4, rows, 384), lambda i: (i, 0, 0)),
        out_shape=jax.ShapeDtypeStruct((2 * count, rows, 384), BF16),
        compiler_params=VMEM,
        name="pack_cotangent",
    )(cotangent, after)


def transform_first(table_ref, data_ref, spec_ref):
    count, _, lanes = data_ref.shape

    def one(j, carry):
        start = pl.ds(pl.multiple_of(16 * j, 16), 16)
        block = data_ref[:, start, :].reshape(count * 16, lanes)
        part = dot(table_ref[j], block).astype(BF16)
        spec_ref[:, start, :] = part.reshape(2 * FREQ_ROWS, 16, lanes)
        return carry

    lax.fori_loop(0, 8, one, 0)


def frequency_weight(k1):
    edge = jnp.logical_or(k1 == 0, k1 == FREQ_ROWS - 1)
    return jnp.where(edge, 1.0 / 4096.0, 2.0 / 4096.0).astype(F32)


def make_filter_kernel(
    feat_ref,
    fin_ref,
    bias_ref,
    mid_ref,
    fout_ref,
    rate_ref,
    table_ref,
    second_ref,
    s1_ref,
    c1_ref,
    s2_ref,
    c2_ref,
    spec_ref,
    taps_ref,
    work_ref,
):
    step_rows = 256
    total = feat_ref.shape[0]

    def one(i, carry):
        rows = pl.ds(pl.multiple_of(i * step_rows, step_rows), step_rows)
        inner = dot(feat_ref[rows, :], fin_ref[...]) + bias_ref[0:1, :]
        s1, c1 = sine_pair(SINE_FREQ * inner)
        s1_ref[rows, :] = s1.astype(BF16)
        c1_ref[rows, :] = c1.astype(BF16)
        p1 = s1.astype(BF16)
        r1 = s1 - p1.astype(F32)
        p2 = r1.astype(BF16)
        p3 = (r1 - p2.astype(F32)).astype(BF16)
        outer = dot(jnp.concatenate([p1, p2, p3], axis=1), mid_ref[...]) + bias_ref[1:2, :]
        s2, c2 = sine_pair(SINE_FREQ * outer)
        s2_ref[rows, :] = s2.astype(BF16)
        c2_ref[rows, :] = c2.astype(BF16)
        q1 = s2.astype(BF16)
        q2 = (s2 - q1.astype(F32)).astype(BF16)
        raw = dot(jnp.concatenate([q1, q2], axis=1), fout_ref[...])
        lag = i * step_rows + lax.broadcasted_iota(jnp.int32, (step_rows, 256), 0)
        signed = jnp.where(lag < total // 2, lag, total - lag)
        distance = signed.astype(F32) * (2.0 / total)
        kernel = raw * jnp.exp(-distance * rate_ref[...])
        taps_ref[pl.ds(2 * i, 2), :, :] = kernel.astype(BF16).reshape(2, COLS, 256)
        return carry

    lax.fori_loop(0, total // step_rows, one, 0)
    transform_first(table_ref, taps_ref, work_ref)

    def second(k1, carry):
        part = work_ref[pl.ds(2 * k1, 2), :, :].reshape(256, 256)
        spec_ref[k1] = dot(second_ref[...], part) * frequency_weight(k1)
        return carry

    lax.fori_loop(0, FREQ_ROWS, second, 0)


def make_filter(feats, fin, bias, mid, fout, rate, table, second):
    total = feats.shape[0]
    hidden = jax.ShapeDtypeStruct((total, 128), BF16)
    return pl.pallas_call(
        make_filter_kernel,
        out_shape=(hidden,) * 4 + (jax.ShapeDtypeStruct((FREQ_ROWS, 256, 256), F32),),
        scratch_shapes=[
            pltpu.VMEM((FULL_ROWS, COLS, 256), BF16),
            pltpu.VMEM((2 * FREQ_ROWS, COLS, 256), BF16),
        ],
        compiler_params=VMEM,
        name="make_filter",
    )(feats, fin, bias, mid, fout, rate, table, second)


def normed_pair(payload, rows, scales, offsets):
    value = payload[:rows].astype(F32)
    stats = to_columns(join_rows(payload[rows:, :rows]))
    mean = spread(stats[:, 0:1], stats[:, 2:3], rows)
    scale = spread(stats[:, 1:2], stats[:, 3:4], rows)
    unit = (value - mean) * scale
    return unit, scale, unit * scales + offsets


def mixer_in_kernel(
    counts_ref, x_ref, scales_ref, offsets_ref, w_ref, taps_ref, masked_ref, short_ref, values_ref, ring_ref, now_ref
):
    rows = values_ref.shape[0]
    step = pl.program_id(0)
    last = pl.num_programs(0) - 1
    count_a, count_b = counts_ref[0], counts_ref[1]

    @pl.when(step == 0)
    def _():
        ring_ref[...] = jnp.zeros_like(ring_ref)

    @pl.when(step < last)
    def _():
        _, _, normed = normed_pair(x_ref[0], rows, scales_ref[...], offsets_ref[...])
        out = dot(stacked(normed).astype(BF16), w_ref[...])
        keep = position_mask(step * rows, rows, count_a, count_b)
        for s in range(3):
            now_ref[s] = packed(out[:, 256 * s : 256 * (s + 1)]) * keep

    @pl.when(step == last)
    def _():
        now_ref[...] = jnp.zeros_like(now_ref)

    for s in range(3):
        ring_ref[s, rows + 8 :, :] = now_ref[s, :8, :]

    @pl.when(step > 0)
    def _():
        shorts = []
        for s in range(3):
            window = ring_ref[s]
            before = window[7 : 7 + rows]
            here = window[8 : 8 + rows]
            after = window[9 : 9 + rows]
            masked_ref[s] = here.astype(BF16)
            short = (
                taps_ref[s : s + 1, :] * before
                + taps_ref[3 + s : 4 + s, :] * here
                + taps_ref[6 + s : 7 + s, :] * after
            )
            short_ref[s] = short.astype(BF16)
            shorts.append(short)
        keep = position_mask((step - 1) * rows, rows, count_a, count_b)
        values_ref[...] = (shorts[2] * shorts[0] * keep).astype(BF16)

    ring_ref[:, 0:8, :] = ring_ref[:, rows : rows + 8, :]
    ring_ref[:, 8 : 8 + rows, :] = now_ref[...]


def lagged(step):
    return jnp.maximum(step - 1, 0)


def mixer_in(counts, payload, scales, offsets, weight, taps, total):
    chunks, tall, _ = payload.shape
    rows = tall - STAT_ROWS
    whole = lambda shape: pl.BlockSpec(shape, lambda i: (0,) * len(shape))
    return pl.pallas_call(
        mixer_in_kernel,
        grid=(chunks + 1,),
        in_specs=[
            pl.BlockSpec(memory_space=pltpu.SMEM),
            pl.BlockSpec((1, tall, 384), lambda i: (jnp.minimum(i, chunks - 1), 0, 0)),
            whole((1, 384)),
            whole((1, 384)),
            whole((256, 768)),
            whole((9, 384)),
        ],
        out_specs=[
            pl.BlockSpec((3, rows, 384), lambda i: (0, lagged(i), 0)),
            pl.BlockSpec((3, rows, 384), lambda i: (0, lagged(i), 0)),
            pl.BlockSpec((rows, 384), lambda i: (lagged(i), 0)),
        ],
        out_shape=[
            jax.ShapeDtypeStruct((3, total, 384), BF16),
            jax.ShapeDtypeStruct((3, total, 384), BF16),
            jax.ShapeDtypeStruct((total, 384), BF16),
        ],
        scratch_shapes=[
            pltpu.VMEM((3, rows + 16, 384), F32),
            pltpu.VMEM((3, rows, 384), F32),
        ],
        compiler_params=VMEM,
        name="mixer_in",
    )(counts, payload, scales, offsets, weight, taps)


def filter_lanes(block):
    return jnp.concatenate([block[:, :128], block], axis=1)


def long_conv_kernel(
    values_ref, gate_ref, filter_ref, first_ref, second_ref, third_ref, fourth_ref, spec_ref, conv_ref, gated_ref, work_ref
):
    transform_first(first_ref, values_ref, work_ref)

    def middle(k1, carry):
        part = work_ref[pl.ds(2 * k1, 2), :, :].reshape(256, 384)
        spec = dot(second_ref[...], part)
        spec_ref[k1] = spec.astype(BF16)
        re, im = spec[:128], spec[128:]
        block = filter_ref[k1]
        fre, fim = filter_lanes(block[:128]), filter_lanes(block[128:])
        prod = jnp.concatenate([re * fre - im * fim, re * fim + im * fre], axis=0).astype(BF16)
        work_ref[pl.ds(2 * k1, 2), :, :] = dot(third_ref[...], prod).astype(BF16).reshape(2, COLS, 384)
        return carry

    lax.fori_loop(0, FREQ_ROWS, middle, 0)

    def last(j, carry):
        start = pl.ds(pl.multiple_of(16 * j, 16), 16)
        part = work_ref[:, start, :].reshape(FREQ_ROWS * 32, 384)
        conv = dot(fourth_ref[j], part)
        conv_ref[:, start, :] = conv.astype(BF16).reshape(HALF_ROWS, 16, 384)
        gate = gate_ref[:, start, :].reshape(256, 384).astype(F32)
        gated_ref[:, start, :] = (conv * gate).astype(BF16).reshape(HALF_ROWS, 16, 384)
        return carry

    lax.fori_loop(0, 8, last, 0)


def full_spec(shape):
    return pl.BlockSpec(shape, lambda i: (0,) * len(shape))


def long_conv(values, short, spectrum, tables):
    first, second, third, fourth = tables
    seq = jax.ShapeDtypeStruct((HALF_ROWS, COLS, 384), BF16)
    cube = (HALF_ROWS, COLS, 384)
    return pl.pallas_call(
        long_conv_kernel,
        grid=(1,),
        in_specs=[
            full_spec(cube),
            pl.BlockSpec((None,) + cube, lambda i: (1, 0, 0, 0)),
            full_spec((FREQ_ROWS, 256, 256)),
            full_spec((8, FREQ_ROWS * 32, 256)),
            full_spec((256, 256)),
            full_spec((256, 256)),
            full_spec((8, 256, FREQ_ROWS * 32)),
        ],
        out_specs=[full_spec((FREQ_ROWS, 256, 384)), full_spec(cube), full_spec(cube)],
        out_shape=[jax.ShapeDtypeStruct((FREQ_ROWS, 256, 384), BF16), seq, seq],
        scratch_shapes=[pltpu.VMEM((2 * FREQ_ROWS, COLS, 384), BF16)],
        compiler_params=VMEM,
        name="long_conv",
    )(
        values.reshape(cube),
        short.reshape((3,) + cube),
        spectrum,
        first,
        second,
        third,
        fourth,
    )


def mixer_out_kernel(x_ref, gated_ref, w_ref, middle_ref, stats_ref):
    rows = gated_ref.shape[0]
    out = packed(dot(stacked(gated_ref[...]), w_ref[...]))
    middle = x_ref[0, :rows, :].astype(F32) + out
    middle_ref[...] = middle
    sum_a, sum_b = pair_sum(middle)
    mean_a, mean_b = sum_a * (1.0 / 192.0), sum_b * (1.0 / 192.0)
    centred = middle - spread(mean_a, mean_b, rows)
    square_a, square_b = pair_sum(centred * centred)
    stats_ref[0] = to_rows((mean_a, square_a, mean_b, square_b), rows)


def mixer_out(payload, gated, weight):
    chunks, tall, _ = payload.shape
    rows = tall - STAT_ROWS
    return pl.pallas_call(
        mixer_out_kernel,
        grid=(chunks,),
        in_specs=[
            pl.BlockSpec((1, tall, 384), lambda i: (i, 0, 0)),
            pl.BlockSpec((rows, 384), lambda i: (i, 0)),
            full_spec((256, 256)),
        ],
        out_specs=[
            pl.BlockSpec((rows, 384), lambda i: (i, 0)),
            pl.BlockSpec((1, 8, rows), lambda i: (i, 0, 0)),
        ],
        out_shape=[
            jax.ShapeDtypeStruct((chunks * rows, 384), F32),
            jax.ShapeDtypeStruct((chunks, 8, rows), F32),
        ],
        compiler_params=VMEM,
        name="mixer_out",
    )(payload, gated, weight)


def column_sums(value):
    return jnp.sum(value.reshape(value.shape[0] // 8, 8, value.shape[1]), axis=0)


def fold_rows(value):
    return jnp.concatenate([value[:128], value[128:192] + value[192:256]], axis=0)


def fold_lanes(value):
    last = value[:, 128:]
    summed = jnp.where(low_lanes(value.shape[0]), last + half_turn(last), jnp.zeros_like(last))
    return jnp.concatenate([value[:, :128], summed], axis=1)


def feed_forward_kernel(
    middle_ref,
    cot_ref,
    s0_ref,
    s1_ref,
    s2_ref,
    s3_ref,
    scales_ref,
    offsets_ref,
    up_ref,
    upt_ref,
    down_ref,
    downt_ref,
    out_ref,
    q_ref,
    sums_ref,
    norm_ref,
    gup_ref,
    gdown_ref,
    small_ref,
    up_acc,
    down_acc,
):
    rows = middle_ref.shape[0]
    step = pl.program_id(0)

    @pl.when(step == 0)
    def _():
        up_acc[...] = jnp.zeros_like(up_acc)
        down_acc[...] = jnp.zeros_like(down_acc)
        small_ref[...] = jnp.zeros_like(small_ref)

    parts = [ref[0] for ref in (s0_ref, s1_ref, s2_ref, s3_ref)]
    mean = (parts[0] + parts[1] + parts[2] + parts[3]) * 0.25
    spread_sum = jnp.zeros_like(mean)
    for part in parts:
        gap = part - mean
        spread_sum += 192.0 * gap * gap
    squares = parts[0] + parts[1] + parts[2] + parts[3]
    scale_a = lax.rsqrt((squares[1:2] + spread_sum[0:1]) * (1.0 / 768.0) + EPS)
    scale_b = lax.rsqrt((squares[3:4] + spread_sum[2:3]) * (1.0 / 768.0) + EPS)
    norm = jnp.concatenate([mean[0:1], scale_a, mean[2:3], scale_b, jnp.zeros((4, rows), F32)], axis=0)
    norm_ref[0] = norm
    columns = to_columns(norm)
    middle = middle_ref[...]
    unit = (middle - spread(columns[:, 0:1], columns[:, 2:3], rows)) * spread(columns[:, 1:2], columns[:, 3:4], rows)
    normed = stacked(unit * scales_ref[...] + offsets_ref[...]).astype(BF16)
    cot = stacked(cot_ref[0])
    normed_t = normed.T
    cot_t = cot.T
    down = jnp.zeros((2 * rows, 256), F32)
    back = jnp.zeros((2 * rows, 256), F32)
    width = 256
    for f in range(768 // width):
        at = slice(width * f, width * (f + 1))
        at_up = slice(768 + width * f, 768 + width * (f + 1))
        gate = dot(normed, up_ref[:, at])
        upper = dot(normed, up_ref[:, at_up])
        grad_hidden = dot(cot, downt_ref[:, at])
        cdf, density = normal_parts(gate)
        active = gate * cdf
        hidden = (active * upper).astype(BF16)
        grad_gate = (grad_hidden * upper * (cdf + gate * density)).astype(BF16)
        grad_upper = (grad_hidden * active).astype(BF16)
        down += dot(hidden, down_ref[at, :])
        back += dot(grad_gate, upt_ref[at, :]) + dot(grad_upper, upt_ref[at_up, :])
        up_acc[:, at] += fold_rows(dot(normed_t, grad_gate))
        up_acc[:, at_up] += fold_rows(dot(normed_t, grad_upper))
        down_acc[:, at] += dot(cot_t, hidden)
    out_ref[0] = (middle + packed(down)).astype(BF16)
    grad = packed(back)
    q = grad * scales_ref[...]
    q_ref[...] = q
    sums_ref[0] = to_rows(pair_sum(q) + pair_sum(q * unit), rows)
    small_ref[0:8, :] += column_sums(grad * unit)
    small_ref[8:16, :] += column_sums(grad)

    @pl.when(step == pl.num_programs(0) - 1)
    def _():
        gup_ref[...] = up_acc[...].astype(BF16)
        gdown_ref[...] = fold_lanes(down_acc[...].T).astype(BF16)


def feed_forward(middle, cot, stats, scales, offsets, up, upt, down, downt):
    chunks, rows, _ = cot.shape
    total = chunks * rows
    stat_spec = pl.BlockSpec((1, 8, rows), lambda i: (i, 0, 0))
    rows_spec = pl.BlockSpec((rows, 384), lambda i: (i, 0))
    chunk_spec = pl.BlockSpec((1, rows, 384), lambda i: (i, 0, 0))
    stat_shape = jax.ShapeDtypeStruct((chunks, 8, rows), F32)
    return pl.pallas_call(
        feed_forward_kernel,
        grid=(chunks,),
        in_specs=[rows_spec, chunk_spec]
        + [stat_spec] * 4
        + [full_spec(a.shape) for a in (scales, offsets, up, upt, down, downt)],
        out_specs=[
            chunk_spec,
            rows_spec,
            stat_spec,
            stat_spec,
            full_spec((192, 1536)),
            full_spec((768, 256)),
            full_spec((16, 384)),
        ],
        out_shape=[
            jax.ShapeDtypeStruct((chunks, rows, 384), BF16),
            jax.ShapeDtypeStruct((total, 384), F32),
            stat_shape,
            stat_shape,
            jax.ShapeDtypeStruct((192, 1536), BF16),
            jax.ShapeDtypeStruct((768, 256), BF16),
            jax.ShapeDtypeStruct((16, 384), F32),
        ],
        scratch_shapes=[pltpu.VMEM((192, 1536), F32), pltpu.VMEM((256, 768), F32)],
        compiler_params=VMEM,
        name="feed_forward",
    )(middle, cot, *stats, scales, offsets, up, upt, down, downt)


def gate_back_kernel(
    q_ref,
    middle_ref,
    cot_ref,
    norm_ref,
    s0_ref,
    s1_ref,
    s2_ref,
    s3_ref,
    gated_ref,
    conv_ref,
    short_ref,
    wt_ref,
    grad_ref,
    grad_conv_ref,
    grad_short_ref,
    gout_ref,
    out_acc,
):
    rows = q_ref.shape[0]
    step = pl.program_id(0)

    @pl.when(step == 0)
    def _():
        out_acc[...] = jnp.zeros_like(out_acc)

    sums = (s0_ref[0] + s1_ref[0] + s2_ref[0] + s3_ref[0]) * (1.0 / 768.0)
    columns = to_columns(sums)
    norm = to_columns(norm_ref[0])
    scale = spread(norm[:, 1:2], norm[:, 3:4], rows)
    unit = (middle_ref[...] - spread(norm[:, 0:1], norm[:, 2:3], rows)) * scale
    mean_q = spread(columns[:, 0:1], columns[:, 1:2], rows)
    mean_qh = spread(columns[:, 2:3], columns[:, 3:4], rows)
    grad = cot_ref[0].astype(F32) + scale * (q_ref[...] - mean_q - unit * mean_qh)
    grad_ref[...] = grad
    branch = stacked(grad).astype(BF16)
    out_acc[...] += fold_rows(dot(stacked(gated_ref[...]).T, branch))
    grad_gated = packed(dot(branch, wt_ref[...]))
    grad_conv_ref[...] = (grad_gated * short_ref[0].astype(F32)).astype(BF16)
    grad_short_ref[...] = (grad_gated * conv_ref[...].astype(F32)).astype(BF16)

    @pl.when(step == pl.num_programs(0) - 1)
    def _():
        gout_ref[...] = fold_lanes(out_acc[...]).astype(BF16)


def gate_back(q, middle, cot, norm, sums, gated, conv, short, wt):
    chunks, rows, _ = cot.shape
    total = chunks * rows
    stat_spec = pl.BlockSpec((1, 8, rows), lambda i: (i, 0, 0))
    rows_spec = pl.BlockSpec((rows, 384), lambda i: (i, 0))
    return pl.pallas_call(
        gate_back_kernel,
        grid=(chunks,),
        in_specs=[
            rows_spec,
            rows_spec,
            pl.BlockSpec((1, rows, 384), lambda i: (i, 0, 0)),
            stat_spec,
            stat_spec,
            stat_spec,
            stat_spec,
            stat_spec,
            rows_spec,
            rows_spec,
            pl.BlockSpec((1, rows, 384), lambda i: (1, i, 0)),
            full_spec((256, 256)),
        ],
        out_specs=[rows_spec, rows_spec, rows_spec, full_spec((192, 256))],
        out_shape=[
            jax.ShapeDtypeStruct((total, 384), F32),
            jax.ShapeDtypeStruct((total, 384), BF16),
            jax.ShapeDtypeStruct((total, 384), BF16),
            jax.ShapeDtypeStruct((192, 256), BF16),
        ],
        scratch_shapes=[pltpu.VMEM((192, 256), F32)],
        compiler_params=VMEM,
        name="gate_back",
    )(q, middle, cot, norm, *sums, gated, conv, short, wt)


def conv_back_kernel(
    grad_ref, spec_ref, filter_ref, first_ref, second_ref, third_ref, fourth_ref, after_ref, out_ref, cross_ref, work_ref
):
    transform_first(first_ref, grad_ref, work_ref)

    def middle(k1, carry):
        part = work_ref[pl.ds(2 * k1, 2), :, :].reshape(256, 384)
        grad = dot(second_ref[...], part)
        re, im = grad[:128], grad[128:]
        spec = spec_ref[k1].astype(F32)
        vre, vim = spec[:128], spec[128:]
        cre = re * vre + im * vim
        cim = im * vre - re * vim
        weight = frequency_weight(k1)
        fold = lambda v: jnp.concatenate([v[:, :128] + v[:, 128:256], v[:, 256:]], axis=1)
        cross_ref[k1] = (jnp.concatenate([fold(cre), fold(cim)], axis=0) * weight).astype(BF16)
        block = filter_ref[k1]
        fre, fim = filter_lanes(block[:128]), filter_lanes(block[128:])
        prod = jnp.concatenate([re * fre + im * fim, im * fre - re * fim], axis=0).astype(BF16)
        work_ref[pl.ds(2 * k1, 2), :, :] = dot(third_ref[...], prod).astype(BF16).reshape(2, COLS, 384)
        return carry

    lax.fori_loop(0, FREQ_ROWS, middle, 0)

    def last(j, carry):
        start = pl.ds(pl.multiple_of(16 * j, 16), 16)
        part = work_ref[:, start, :].reshape(FREQ_ROWS * 32, 384)
        out_ref[:, start, :] = dot(fourth_ref[j], part).reshape(HALF_ROWS, 16, 384)
        return carry

    lax.fori_loop(0, 8, last, 0)


def conv_back(grad, spec, spectrum, tables, after):
    first, second, third, fourth = tables
    cube = (HALF_ROWS, COLS, 384)
    return pl.pallas_call(
        conv_back_kernel,
        grid=(1,),
        in_specs=[
            full_spec(cube),
            full_spec((FREQ_ROWS, 256, 384)),
            full_spec((FREQ_ROWS, 256, 256)),
            full_spec((8, FREQ_ROWS * 32, 256)),
            full_spec((256, 256)),
            full_spec((256, 256)),
            full_spec((8, 256, FREQ_ROWS * 32)),
            pl.BlockSpec(memory_space=pl.ANY),
        ],
        out_specs=[full_spec(cube), full_spec((FREQ_ROWS, 256, 256))],
        out_shape=[
            jax.ShapeDtypeStruct(cube, F32),
            jax.ShapeDtypeStruct((FREQ_ROWS, 256, 256), BF16),
        ],
        scratch_shapes=[pltpu.VMEM((2 * FREQ_ROWS, COLS, 384), BF16)],
        compiler_params=VMEM,
        name="conv_back",
    )(grad.reshape(cube), spec, spectrum, first, second, third, fourth, after)


def mixer_back_kernel(
    counts_ref,
    grad_values_ref,
    grad_one_ref,
    short_a_ref,
    short_b_ref,
    masked_ref,
    x_ref,
    grad_ref,
    scales_ref,
    offsets_ref,
    taps_ref,
    wt_ref,
    after_ref,
    out_ref,
    gin_ref,
    small_ref,
    in_acc,
    ring_ref,
    now_ref,
):
    rows = grad_ref.shape[0]
    step = pl.program_id(0)
    last = pl.num_programs(0) - 1
    count_a, count_b = counts_ref[0], counts_ref[1]

    @pl.when(step == 0)
    def _():
        ring_ref[...] = jnp.zeros_like(ring_ref)
        in_acc[...] = jnp.zeros_like(in_acc)
        small_ref[...] = jnp.zeros_like(small_ref)

    @pl.when(step < last)
    def _():
        keep = position_mask(step * rows, rows, count_a, count_b)
        grad_values = grad_values_ref[...] * keep
        now_ref[0] = grad_values * short_b_ref[0].astype(F32)
        now_ref[1] = grad_one_ref[...].astype(F32)
        now_ref[2] = grad_values * short_a_ref[0].astype(F32)

    @pl.when(step == last)
    def _():
        now_ref[...] = jnp.zeros_like(now_ref)

    for s in range(3):
        ring_ref[s, rows + 8 :, :] = now_ref[s, :8, :]

    @pl.when(step > 0)
    def _():
        keep = position_mask((step - 1) * rows, rows, count_a, count_b)
        grads = []
        for s in range(3):
            window = ring_ref[s]
            shifted = (window[9 : 9 + rows], window[8 : 8 + rows], window[7 : 7 + rows])
            masked = masked_ref[s].astype(F32)
            total = jnp.zeros((rows, 384), F32)
            for j in range(3):
                total += taps_ref[3 * j + s : 3 * j + s + 1, :] * shifted[j]
                at = 16 + 8 * (3 * j + s)
                small_ref[at : at + 8, :] += column_sums(shifted[j] * masked)
            grads.append(stacked(total * keep).astype(BF16))
        flat = jnp.concatenate(grads, axis=1)
        unit, scale, normed = normed_pair(x_ref[0], rows, scales_ref[...], offsets_ref[...])
        in_acc[...] += fold_rows(dot(stacked(normed).astype(BF16).T, flat))
        grad_normed = packed(dot(flat, wt_ref[...]))
        small_ref[0:8, :] += column_sums(grad_normed * unit)
        small_ref[8:16, :] += column_sums(grad_normed)
        q = grad_normed * scales_ref[...]
        out_ref[0, :rows, :] = (grad_ref[...] + scale * q).astype(BF16)
        out_ref[0, rows:, :rows] = split_rows(to_rows(pair_sum(q) + pair_sum(q * unit), rows))

    ring_ref[:, 0:8, :] = ring_ref[:, rows : rows + 8, :]
    ring_ref[:, 8 : 8 + rows, :] = now_ref[...]

    @pl.when(step == last)
    def _():
        grads = in_acc[...]
        for s in range(3):
            gin_ref[:, 256 * s : 256 * (s + 1)] = fold_lanes(grads[:, 256 * s : 256 * (s + 1)]).astype(BF16)


def mixer_back(counts, grad_values, grad_one, short, masked, payload, grad, scales, offsets, taps, wt, after):
    chunks, tall, _ = payload.shape
    rows = tall - STAT_ROWS
    ahead = lambda i: jnp.minimum(i, chunks - 1)
    return pl.pallas_call(
        mixer_back_kernel,
        grid=(chunks + 1,),
        in_specs=[
            pl.BlockSpec(memory_space=pltpu.SMEM),
            pl.BlockSpec((rows, 384), lambda i: (ahead(i), 0)),
            pl.BlockSpec((rows, 384), lambda i: (ahead(i), 0)),
            pl.BlockSpec((1, rows, 384), lambda i: (0, ahead(i), 0)),
            pl.BlockSpec((1, rows, 384), lambda i: (2, ahead(i), 0)),
            pl.BlockSpec((3, rows, 384), lambda i: (0, lagged(i), 0)),
            pl.BlockSpec((1, tall, 384), lambda i: (lagged(i), 0, 0)),
            pl.BlockSpec((rows, 384), lambda i: (lagged(i), 0)),
            full_spec((1, 384)),
            full_spec((1, 384)),
            full_spec((9, 384)),
            full_spec((768, 256)),
            pl.BlockSpec(memory_space=pl.ANY),
        ],
        out_specs=[
            pl.BlockSpec((1, tall, 384), lambda i: (lagged(i), 0, 0)),
            full_spec((192, 768)),
            full_spec((88, 384)),
        ],
        out_shape=[
            jax.ShapeDtypeStruct((chunks, tall, 384), BF16),
            jax.ShapeDtypeStruct((192, 768), BF16),
            jax.ShapeDtypeStruct((88, 384), F32),
        ],
        scratch_shapes=[
            pltpu.VMEM((192, 768), F32),
            pltpu.VMEM((3, rows + 16, 384), F32),
            pltpu.VMEM((3, rows, 384), F32),
        ],
        compiler_params=VMEM,
        name="mixer_back",
    )(counts, grad_values, grad_one, short, short, masked, payload, grad, scales, offsets, taps, wt, after)


def filter_back_kernel(
    cross_ref,
    s1_ref,
    c1_ref,
    s2_ref,
    c2_ref,
    feat_ref,
    midt_ref,
    foutt_ref,
    rate_ref,
    third_ref,
    fourth_ref,
    after_ref,
    gfin_ref,
    gmid_ref,
    gfout_ref,
    gbias_ref,
    work_ref,
    taps_ref,
):
    total = feat_ref.shape[0]
    step_rows = 256

    def second(k1, carry):
        work_ref[pl.ds(2 * k1, 2), :, :] = dot(third_ref[...], cross_ref[k1]).astype(BF16).reshape(2, COLS, 256)
        return carry

    lax.fori_loop(0, FREQ_ROWS, second, 0)

    def last(j, carry):
        start = pl.ds(pl.multiple_of(16 * j, 16), 16)
        part = work_ref[:, start, :].reshape(FREQ_ROWS * 32, 256)
        taps_ref[:, start, :] = dot(fourth_ref[j], part).reshape(FULL_ROWS, 16, 256)
        return carry

    lax.fori_loop(0, 8, last, 0)
    gfin_ref[...] = jnp.zeros_like(gfin_ref)
    gmid_ref[...] = jnp.zeros_like(gmid_ref)
    gfout_ref[...] = jnp.zeros_like(gfout_ref)
    gbias_ref[...] = jnp.zeros_like(gbias_ref)

    def one(i, carry):
        rows = pl.ds(pl.multiple_of(i * step_rows, step_rows), step_rows)
        lag = i * step_rows + lax.broadcasted_iota(jnp.int32, (step_rows, 256), 0)
        signed = jnp.where(lag < total // 2, lag, total - lag)
        distance = signed.astype(F32) * (2.0 / total)
        grad = taps_ref[pl.ds(2 * i, 2), :, :].reshape(step_rows, 256) * jnp.exp(-distance * rate_ref[...])
        grad = grad.astype(BF16)
        gfout_ref[...] += dot(s2_ref[rows, :].T, grad)
        grad_second = dot(grad, foutt_ref[...]) * (SINE_FREQ * c2_ref[rows, :].astype(F32))
        gbias_ref[8:16, :] += column_sums(grad_second)
        grad_second = grad_second.astype(BF16)
        gmid_ref[...] += dot(s1_ref[rows, :].T, grad_second)
        grad_first = dot(grad_second, midt_ref[...]) * (SINE_FREQ * c1_ref[rows, :].astype(F32))
        gbias_ref[0:8, :] += column_sums(grad_first)
        gfin_ref[...] += dot(feat_ref[rows, :].T, grad_first.astype(BF16))
        return carry

    lax.fori_loop(0, total // step_rows, one, 0)


def filter_back(cross, hidden, feats, midt, foutt, rate, third, fourth, after):
    vmem = pl.BlockSpec(memory_space=pltpu.VMEM)
    return pl.pallas_call(
        filter_back_kernel,
        in_specs=[vmem] * 11 + [pl.BlockSpec(memory_space=pl.ANY)],
        out_shape=[
            jax.ShapeDtypeStruct((16, 128), F32),
            jax.ShapeDtypeStruct((128, 128), F32),
            jax.ShapeDtypeStruct((128, 256), F32),
            jax.ShapeDtypeStruct((16, 128), F32),
        ],
        scratch_shapes=[
            pltpu.VMEM((2 * FREQ_ROWS, COLS, 256), BF16),
            pltpu.VMEM((FULL_ROWS, COLS, 256), F32),
        ],
        compiler_params=VMEM,
        name="filter_back",
    )(cross, *hidden, feats, midt, foutt, rate, third, fourth, after)


def unpack_out_kernel(x_ref, out_ref):
    for even in (0, 2):
        a, b = unpack_pairs(x_ref[even].astype(F32), x_ref[even + 1].astype(F32))
        out_ref[0, :, 192 * even : 192 * even + 384] = a.astype(BF16)
        out_ref[1, :, 192 * even : 192 * even + 384] = b.astype(BF16)


def unpack_out(value):
    chunks, rows, _ = value.shape
    return pl.pallas_call(
        unpack_out_kernel,
        grid=(chunks // 4,),
        in_specs=[pl.BlockSpec((4, rows, 384), lambda i: (i, 0, 0))],
        out_specs=pl.BlockSpec((2, rows, 768), lambda i: (i, 0, 0)),
        out_shape=jax.ShapeDtypeStruct((chunks // 2, rows, 768), BF16),
        compiler_params=VMEM,
        name="unpack_out",
    )(value)


def unpack_grad_kernel(x_ref, tokens_ref, out_ref):
    rows = tokens_ref.shape[1]
    sums = jnp.zeros((8, rows), F32)
    for block in range(4):
        sums += join_rows(x_ref[block, rows:, :rows])
    columns = to_columns(sums) * (1.0 / 768.0)
    wide = ([], [])
    for even in (0, 2):
        a, b = unpack_pairs(x_ref[even, :rows].astype(F32), x_ref[even + 1, :rows].astype(F32))
        wide[0].append(a)
        wide[1].append(b)
    for which in range(2):
        token = tokens_ref[which].astype(F32)
        mean, scale = row_stats(token)
        unit = (token - mean) * scale
        grad = jnp.concatenate(wide[which], axis=1)
        mean_q = columns[:, which : which + 1]
        mean_qh = columns[:, 2 + which : 3 + which]
        out_ref[which] = grad - scale * (mean_q + unit * mean_qh)


def unpack_grad(value, tokens):
    chunks, tall, _ = value.shape
    rows = tall - STAT_ROWS
    return pl.pallas_call(
        unpack_grad_kernel,
        grid=(chunks // 4,),
        in_specs=[
            pl.BlockSpec((4, tall, 384), lambda i: (i, 0, 0)),
            pl.BlockSpec((2, rows, 768), lambda i: (i, 0, 0)),
        ],
        out_specs=pl.BlockSpec((2, rows, 768), lambda i: (i, 0, 0)),
        out_shape=jax.ShapeDtypeStruct((chunks // 2, rows, 768), F32),
        compiler_params=VMEM,
        name="unpack_grad",
    )(value, tokens)


def doubled(value, axis):
    return jnp.concatenate([value, lax.slice_in_dim(value, 128, 192, axis=axis)], axis=axis)


def pair_lanes(value):
    head, tail = value[:, :128], value[:, 128:]
    return jnp.concatenate([head, head, tail, tail], axis=1)


def unpair_lanes(value):
    return jnp.concatenate([value[:, :128] + value[:, 128:256], value[:, 256:320] + value[:, 320:]], axis=1)


def at_block(value, block, axis):
    return lax.dynamic_index_in_dim(value, block, axis=axis, keepdims=False)


def per_device(
    tokens,
    lengths,
    cotangent,
    norm_gain,
    norm_bias,
    in_weight,
    conv_taps,
    filter_in,
    filter_mid,
    filter_bias,
    filter_out,
    out_weight,
    up_weight,
    down_weight,
):
    count, rows, features = tokens.shape
    blocks = in_weight.shape[1]
    data_size = lax.axis_size("dp")
    seq_size = lax.axis_size("seq")
    total = rows * seq_size
    groups = seq_size // blocks
    place = lax.axis_index("seq")
    block = place % blocks
    group = place // blocks
    width = features // blocks
    data_at = lax.axis_index("dp")

    def exchange(value):
        return lax.all_to_all(value, "seq", 0, 0, tiled=True)

    def shared(value):
        out = [value]
        for r in range(1, blocks):
            out.append(lax.ppermute(value, "seq", [(i, i ^ r) for i in range(seq_size)]))
        return out

    def gathered(value):
        out = [value]
        for r in range(1, data_size):
            out.append(lax.ppermute(value, "dp", [(i, i ^ r) for i in range(data_size)]))
        every = jnp.stack(out)
        return jnp.concatenate([lax.dynamic_slice_in_dim(every, data_at ^ i, 1, axis=0) for i in range(data_size)])

    def from_blocks(value):
        every = jnp.stack(shared(value))
        return jnp.concatenate([lax.dynamic_slice_in_dim(every, block ^ i, 1, axis=0) for i in range(blocks)])

    fout_parts = []
    for q in range(groups):
        pairs = [(groups * (i % blocks) + (i // blocks + q) % groups, i) for i in range(seq_size)]
        fout_parts.append(lax.ppermute(filter_out, "seq", pairs))
    fout_every = jnp.stack(fout_parts)
    fout_block = jnp.concatenate(
        [at_block(fout_every, (i - group) % groups, 0) for i in range(groups)], axis=1
    )

    payload = exchange(pack_tokens(tokens))
    counts = lax.dynamic_slice_in_dim(lengths, 2 * group, 2, axis=0)

    small = jnp.concatenate(
        [
            norm_gain.reshape(-1),
            norm_bias.reshape(-1),
            conv_taps.reshape(-1),
            filter_in.reshape(-1),
            filter_bias.reshape(-1),
            filter_mid.reshape(-1),
            fout_block.reshape(-1),
        ]
    )
    small_size = -(-small.shape[0] // 2048) * 2048
    small = jnp.pad(small, (0, small_size - small.shape[0])).reshape(-1, 128)
    small_all = gathered(small).reshape(data_size, small_size)
    shard = features // data_size
    hidden_shard = filter_in.shape[1]
    cuts = np.cumsum(
        [0, 2 * shard, 2 * shard, 9 * shard, 5 * hidden_shard, 2 * hidden_shard, 128 * hidden_shard, width * hidden_shard]
    )
    pieces = [small_all[:, cuts[i] : cuts[i + 1]] for i in range(7)]

    def channels(piece, lead):
        whole = jnp.moveaxis(piece.reshape(data_size, lead, shard), 0, 1).reshape(lead, features)
        return lax.dynamic_slice_in_dim(whole, block * width, width, axis=1).astype(F32)

    gains = pair_lanes(channels(pieces[0], 2))
    offsets = pair_lanes(channels(pieces[1], 2))
    taps = pair_lanes(channels(pieces[2], 9))
    fin = jnp.moveaxis(pieces[3].reshape(data_size, 5, hidden_shard), 0, 1).reshape(5, 128)
    fbias = jnp.moveaxis(pieces[4].reshape(data_size, 2, hidden_shard), 0, 1).reshape(2, 128)
    fmid = pieces[5].reshape(128, 128)
    fout = doubled(pieces[6].reshape(128, width), 1)
    fin_stack = jnp.concatenate([fin, fin, fin, jnp.zeros((1, 128), BF16)], axis=0)
    channel_ids = block * width + jnp.arange(width, dtype=jnp.int32)
    fast, slow = math.log(100.0) / 0.3, math.log(100.0) / 1.5
    rates = slow + (fast - slow) * channel_ids.astype(F32) / float(features - 1)
    rates = doubled(rates[None, :], 1)

    large = jnp.concatenate(
        [
            at_block(in_weight, block, 1).reshape(-1, width),
            at_block(out_weight, block, 0).reshape(-1, width),
            at_block(up_weight, block, 1).reshape(-1, width),
            at_block(down_weight, block, 0).reshape(-1, width),
        ],
        axis=0,
    )
    large_all = lax.all_gather(large, "dp", axis=0, tiled=False)
    part = width // data_size
    row_cuts = np.cumsum([0, 3 * part, part, 8 * part, 4 * part])
    lw = [large_all[:, row_cuts[i] : row_cuts[i + 1]] for i in range(4)]
    w_in = jnp.moveaxis(lw[0].reshape(data_size, 3, part, width), 0, 1).reshape(3, width, width)
    w_in = doubled(doubled(w_in, 2), 1)
    w_in_flat = jnp.moveaxis(w_in, 0, 1).reshape(256, 768)
    w_in_t = jnp.swapaxes(w_in, 1, 2).reshape(768, 256)
    w_out = doubled(doubled(lw[1].reshape(width, width), 1), 0)
    w_up = jnp.moveaxis(lw[2].reshape(data_size, 2, part, 4 * width), 0, 1).reshape(2, width, 4 * width)
    w_up = doubled(w_up, 1)
    w_up_flat = jnp.concatenate([w_up[0], w_up[1]], axis=1)
    w_up_t = jnp.swapaxes(w_up, 1, 2).reshape(8 * width, 256)
    w_down = doubled(lw[3].reshape(4 * width, width), 1)

    first_np, second_np = stage_tables()
    full_first = jnp.asarray(first_np, BF16)
    full_last = jnp.asarray(np.swapaxes(first_np, 1, 2), BF16)
    second = jnp.asarray(second_np, BF16)
    third = jnp.asarray(second_np.T, BF16)
    tables = (full_first[:, :, :256], second, third, full_last[:, :256])
    feats = jnp.asarray(lag_table(total), BF16)

    hidden = make_filter(
        feats,
        fin_stack,
        fbias.astype(F32),
        jnp.concatenate([fmid, fmid, fmid], axis=0),
        jnp.concatenate([fout, fout], axis=0),
        rates,
        full_first,
        second,
    )
    spectrum = hidden[4]
    hidden = hidden[:4]

    cot = exchange(pack_cotangent(cotangent, payload))
    masked, short, values = mixer_in(counts, payload, gains[0:1], offsets[0:1], w_in_flat, taps, total)
    spec, conv, gated = long_conv(values, short, spectrum, tables)
    conv = conv.reshape(total, 384)
    gated = gated.reshape(total, 384)
    middle, stats = mixer_out(payload, gated, w_out)

    out, q, sums, norm, g_up, g_down, small_two = feed_forward(
        middle, cot, shared(stats), gains[1:2], offsets[1:2], w_up_flat, w_up_t, w_down, w_down.T
    )
    ffn = jnp.concatenate(
        [
            g_up.reshape(data_size, part * 8 * width // 256, 256),
            g_down.reshape(data_size, 4 * width // data_size, 256),
        ],
        axis=1,
    )
    ffn = lax.all_to_all(ffn, "dp", 0, 0, tiled=True)
    out = exchange(out)

    grad, grad_conv, grad_one, g_out = gate_back(q, middle, cot, norm, shared(sums), gated, conv, short, w_out.T)
    grad_values, cross = conv_back(grad_conv, spec, spectrum, tables, ffn)
    back, g_in, small_one = mixer_back(
        counts,
        grad_values.reshape(total, 384),
        grad_one,
        short,
        masked,
        payload,
        grad,
        gains[0:1],
        offsets[0:1],
        taps,
        w_in_t,
        out,
    )
    back = exchange(back)
    out_tokens = unpack_out(out)
    grad_tokens = unpack_grad(back, tokens)
    g_fin, g_mid, g_fout, g_fbias = filter_back(cross, hidden, feats, fmid.T, fout.T, rates, third, full_last, out)

    def reduced(value):
        value = value.astype(F32).sum(axis=0)
        step = 1
        while step < groups:
            pairs = [(i, i ^ (step * blocks)) for i in range(seq_size)]
            sent = value.astype(BF16)
            value = sent.astype(F32) + lax.ppermute(sent, "seq", pairs).astype(F32)
            step *= 2
        return from_blocks(value.astype(BF16)).astype(F32)

    ffn = reduced(ffn)
    cut = part * 8 * width // 256
    grad_up = jnp.moveaxis(ffn[:, :cut].reshape(blocks, part, 2, 4 * width), 2, 0)
    grad_down = ffn[:, cut:, :width]

    sums_one = unpair_lanes(small_one.reshape(11, 8, 384).sum(axis=1))
    sums_two = unpair_lanes(small_two.reshape(2, 8, 384).sum(axis=1))
    per_block = jnp.concatenate([sums_one[0:1], sums_two[0:1], sums_one[1:2], sums_two[1:2], sums_one[2:]], axis=0)
    g_fin = g_fin[0:5] + g_fin[5:10] + g_fin[10:15]
    g_fbias = g_fbias.reshape(2, 8, 128).sum(axis=1)
    g_fout = g_fout[:, :192] + jnp.pad(g_fout[:, 192:], ((0, 0), (128, 0)))
    same = jnp.concatenate([per_block.reshape(-1), g_fin.reshape(-1), g_fbias.reshape(-1)])
    own = jnp.concatenate(
        [
            g_in.reshape(data_size, -1),
            g_out.reshape(data_size, -1),
            g_mid.reshape(data_size, -1).astype(BF16),
            g_fout.reshape(data_size, -1).astype(BF16),
            jnp.broadcast_to(same.astype(BF16)[None], (data_size, same.shape[0])),
        ],
        axis=1,
    )
    filled = -(-own.shape[1] // 2048) * 2048
    own = jnp.pad(own, ((0, 0), (0, filled - own.shape[1]))).reshape(data_size, filled // 128, 128)
    rest = reduced(lax.all_to_all(own, "dp", 0, 0, tiled=True)).reshape(blocks, filled)
    ends = np.cumsum(
        [0, part * 768, part * 256, hidden_shard * 128, hidden_shard * width, 13 * width, 5 * 128, 2 * 128]
    )
    got = [rest[:, ends[i] : ends[i + 1]] for i in range(7)]
    grad_in = jnp.moveaxis(got[0].reshape(blocks, part, 3, 256)[..., :width], 2, 0)
    grad_outw = got[1].reshape(blocks, part, 256)[..., :width]
    grad_mid = got[2].reshape(blocks, hidden_shard, 128).sum(axis=0)
    grad_fout = jnp.moveaxis(got[3].reshape(blocks, hidden_shard, width), 0, 1).reshape(hidden_shard, features)
    grad_fout = lax.dynamic_slice_in_dim(grad_fout, place * (features // seq_size), features // seq_size, axis=1)
    norms = jnp.moveaxis(got[4].reshape(blocks, 13, width), 0, 1).reshape(13, features)
    norms = lax.dynamic_slice_in_dim(norms, data_at * shard, shard, axis=1)
    grad_fin = got[5].reshape(blocks, 5, 128).sum(axis=0)
    grad_fin = lax.dynamic_slice_in_dim(grad_fin, data_at * hidden_shard, hidden_shard, axis=1)
    grad_fbias = got[6].reshape(blocks, 2, 128).sum(axis=0)
    grad_fbias = lax.dynamic_slice_in_dim(grad_fbias, data_at * hidden_shard, hidden_shard, axis=1)
    return (
        out_tokens,
        grad_tokens,
        norms[0:2],
        norms[2:4],
        grad_in,
        norms[4:13].reshape(3, 3, shard),
        grad_fin,
        grad_mid,
        grad_fbias,
        grad_fout,
        grad_outw,
        grad_up,
        grad_down,
    )


def solution(mesh):
    placed = (
        P("dp", "seq", None),
        P("dp"),
        P("dp", "seq", None),
        P(None, "dp"),
        P(None, "dp"),
        P(None, None, "dp", None),
        P(None, None, "dp"),
        P(None, "dp"),
        P("dp", None),
        P(None, "dp"),
        P("dp", "seq"),
        P(None, "dp", None),
        P(None, None, "dp", None),
        P(None, "dp", None),
    )
    return jax.shard_map(
        per_device,
        mesh=mesh,
        in_specs=placed,
        out_specs=(
            P("dp", "seq", None),
            P("dp", "seq", None),
            P(None, "dp"),
            P(None, "dp"),
            P(None, None, "dp", None),
            P(None, None, "dp"),
            P(None, "dp"),
            P("dp", None),
            P(None, "dp"),
            P("dp", "seq"),
            P(None, "dp", None),
            P(None, None, "dp", None),
            P(None, "dp", None),
        ),
        check_vma=False,
    )
```

time: 2450 us -> 427 us (0.17)
  matrix products: 775 us -> 0 us
  local copies, waits for them, and re-layouts: 524 us -> 46.9 us
  other arithmetic: 377 us -> 20.5 us
  blocking collectives: 280 us -> 16.2 us
  waiting for transfers between devices: 309 us -> 82 us
  Pallas kernels: 0 us -> 189 us
  starting transfers between devices: 145 us -> 55.7 us
    dot_general x224 -> x0, matrix products: 775 us -> none  [the longest x96 302 us: right_mul(): return jnp.einsum('...kc,cj->...kj', values, table, precision=HIGH)]
    all_gather x36 -> x0, blocking collectives: 241 us -> none  [the longest x4 48.2 us: collect(): lax.all_gather(in_weight, 'dp', axis=2, tiled=True)]
    pallas_call x0 -> x13, Pallas kernels: none -> 189 us  [the longest x1 35.2 us: feed_forward(): pl.pallas_call(feed_forward_kernel, grid=(chunks,), in_specs=[rows_spec,...]
    while x1010 -> x0, local copies, waits for them, and re-layouts: 179 us -> none
    unnamed x19 -> x1, waiting for transfers between devices: 141 us -> 0.02 us
    reduce_scatter x4 -> x0, waiting for transfers between devices: 105 us -> none  [the longest x1 35.6 us: per_device(): lax.psum_scatter(summed[8].astype(jnp.bfloat16), 'dp', scatter_dimension=...]
    while x8 -> x0, other arithmetic: 104 us -> none
    convert_element_type x78 -> x9, other arithmetic: 99.1 us -> 5.36 us  [the longest x4 3.35 us: reduced(): return from_blocks(value.astype(BF16)).astype(F32)]
  transfers between devices with their start and end apart: 52 -> 25, of which waited for: 16 -> 11; matrix products, arithmetic and copies ran while one was open for 39% -> 13% of each run, Pallas kernels for 0% -> 34%
where the time goes in v1:
time: 427 us; the launch traced here: 425 us
  Pallas kernels  189 us (44%)
  waiting for transfers between devices  82 us (19%)
  starting transfers between devices  55.7 us (13%)
  local copies, waits for them, and re-layouts  46.9 us (11%)
  other arithmetic  20.5 us (5%)
  blocking collectives  16.2 us (4%)
  between operations  14.9 us (3%)
    pallas_call x1, Pallas kernels, feed_forward(): pl.pallas_call(feed_forward_kernel, grid=(chunks,), in_specs=[rows_spec,...  35.2 us
    all_to_all x4, waiting for transfers between devices, exchange(): return lax.all_to_all(value, 'seq', 0, 0, tiled=True)  26.9 us
    all_to_all x4, starting transfers between devices, exchange(): return lax.all_to_all(value, 'seq', 0, 0, tiled=True)  25.3 us
    pallas_call x1, Pallas kernels, mixer_back(): pl.pallas_call(mixer_back_kernel, grid=(chunks + 1,), in_specs=[pl.BlockS...  24.1 us
    pallas_call x1, Pallas kernels, make_filter(): pl.pallas_call(make_filter_kernel, out_shape=(hidden,) * 4 + (jax.ShapeDt...  22.6 us
    ppermute x12, waiting for transfers between devices, shared(): lax.ppermute(value, 'seq', [(i, i ^ r) for i in range(seq_size)])  21.8 us
    pallas_call x1, Pallas kernels, conv_back(): pl.pallas_call(conv_back_kernel, grid=(1,), in_specs=[full_spec(cube), fu...  21 us
    ppermute x2, waiting for transfers between devices, per_device(): fout_parts.append(lax.ppermute(filter_out, 'seq', pairs))  20.2 us
  transfers between devices with their start and end apart: 25, of which 11 were waited for; matrix products, arithmetic and copies ran while one was open for 13% of the time, Pallas kernels for 34%

profile of v1, /device:TPU:0, one launch (start us, length us, event | category | flops | bytes accessed | tf_op | source)
XLA Modules:
  0.0 425.3 jit_solution(4001351981589021032)
XLA Ops:
  10.6 7.4 %all-to-all-start = ((bf16[8,272,384]{2,1,0:T(8,128)(2,1)}), bf16[8,272,384]{2,1,0:T(8,128)(2,1)S(1)}, u32[]{:S(2)}, u32[]{:S(2)}) async-start(bf16[8,272,384]{2,1,0:T(8,128)(2,1)} %pack_tokens.1), calls=%async_computation | async-start | bytes 3342336 | tf_op jit(solution)/shard_map/all_to_all | solution.py:1149
  25.9 20.2 %collective-permute-done.1 = bf16[32,96]{1,0:T(8,128)(2,1)S(1)} collective-permute-done((bf16[32,96]{1,0:T(8,128)(2,1)S(1)}, bf16[32,96]{1,0:T(8,128)(2,1)S(1)}, u32[]{:S(2)}, u32[]{:S(2)}) %collective-permute-start.1) | collective-permute-done | bytes 6176 | tf_op jit(solution)/shard_map/ppermute | solution.py:1171
  50.6 6.8 %all-to-all-done.x_ref.after_ref = bf16[8,272,384]{2,1,0:T(8,128)(2,1)S(1)} async-done(((bf16[8,272,384]{2,1,0:T(8,128)(2,1)}), bf16[8,272,384]{2,1,0:T(8,128)(2,1)S(1)}, u32[]{:S(2)}, u32[]{:S(2)}) %all-to-all-start) | async-done | bytes 1671200 | tf_op jit(solution)/shard_map/all_to_all | solution.py:1149
  61.2 8.9 %all-to-all-start.1 = ((bf16[8,256,384]{2,1,0:T(8,128)(2,1)}), bf16[8,256,384]{2,1,0:T(8,128)(2,1)S(1)}, u32[]{:S(2)}, u32[]{:S(2)}) async-start(bf16[8,256,384]{2,1,0:T(8,128)(2,1)} %pack_cotangent.1), calls=%async_computation.1 | async-start | bytes 3145728 | tf_op jit(solution)/shard_map/all_to_all | solution.py:1149
  74.6 22.6 %make_filter.1 = (bf16[4096,128]{1,0:T(8,128)(2,1)}, bf16[4096,128]{1,0:T(8,128)(2,1)}, bf16[4096,128]{1,0:T(8,128)(2,1)}, bf16[4096,128]{1,0:T(8,128)(2,1)}, f32[17,256,256]{2,1,0:T(8,128)}) custom-call(bf16[4096,16]{1,0:T(8,128)(2,1)} %constant.110.clone.feat_ref, bf16[16,128]{1,0:T(8,128)(2,1)} %maximum_maximum_fusion.1.fin_ref, ...), custom_call_target="tpu_custom_call" | custom-call | tf_op jit(solution)/shard_map/make_filter/pallas_call | solution.py:351
  111.6 14.8 %mixer_in.1 = (bf16[3,2048,384]{2,1,0:T(8,128)(2,1)}, bf16[3,2048,384]{2,1,0:T(8,128)(2,1)}, bf16[2048,384]{1,0:T(8,128)(2,1)}) custom-call(s32[2]{0:T(128)} %dynamic_slice.83.counts_ref, bf16[8,272,384]{2,1,0:T(8,128)(2,1)} %copy-done.2, f32[1,384]{1,0:T(1,128)} %get-tuple-element.136.scales_ref, f32[1,384]{1,0:T(1,128)} %get-tuple-element.134.offsets_ref, ...), custom_call_target="tpu_custom_call" | custom-call | tf_op jit(solution)/shard_map/mixer_in/pallas_call | solution.py:430
  126.4 19.8 %long_conv.1 = (bf16[17,256,384]{2,1,0:T(8,128)(2,1)}, bf16[16,128,384]{2,1,0:T(8,128)(2,1)}, bf16[16,128,384]{2,1,0:T(8,128)(2,1)}) custom-call(bf16[16,128,384]{2,1,0:T(8,128)(2,1)} %bitcast.179, bf16[3,16,128,384]{3,2,1,0:T(8,128)(2,1)} %bitcast.131, f32[17,256,256]{2,1,0:T(8,128)} %get-tuple-element.48.filter_ref, ...), custom_call_target="tpu_custom_call" | custom-call | tf_op jit(solution)/shard_map/long_conv/pallas_call | solution.py:502
  146.2 7.3 %mixer_out.1 = (f32[2048,384]{1,0:T(8,128)}, f32[8,8,256]{2,1,0:T(8,128)}) custom-call(bf16[8,272,384]{2,1,0:T(8,128)(2,1)} %copy-done.2, bf16[2048,384]{1,0:T(8,128)(2,1)} %bitcast.163, bf16[256,256]{1,0:T(8,128)(2,1)} %copy.80.w_ref), custom_call_target="tpu_custom_call" | custom-call | tf_op jit(solution)/shard_map/mixer_out/pallas_call | solution.py:545
  162.6 35.2 %feed_forward.1 = (bf16[8,256,384]{2,1,0:T(8,128)(2,1)}, f32[2048,384]{1,0:T(8,128)}, f32[8,8,256]{2,1,0:T(8,128)}, f32[8,8,256]{2,1,0:T(8,128)}, bf16[192,1536]...) custom-call(f32[2048,384]{1,0:T(8,128)} %get-tuple-element.50.middle_ref, ...), custom_call_target="tpu_custom_call" | custom-call | tf_op jit(solution)/shard_map/feed_forward/pallas_call | solution.py:670
  200.8 16.2 %all_to_all.30.after_ref = bf16[4,480,256]{2,1,0:T(8,128)(2,1)S(1)} all-to-all(bf16[4,480,256]{2,1,0:T(8,128)(2,1)S(1)} %pad_maximum_fusion.1), channel_id=1, replica_groups=mesh['dp'=4,'seq'=8] {'dp'}, dimensions={0} | all-to-all | bytes 1966080 | tf_op jit(solution)/shard_map/all_to_all | solution.py:1280
  216.9 4.7 %all-to-all-start.2 = ((bf16[8,256,384]{2,1,0:T(8,128)(2,1)}), bf16[8,256,384]{2,1,0:T(8,128)(2,1)S(1)}, u32[]{:S(2)}, u32[]{:S(2)}) async-start(bf16[8,256,384]{2,1,0:T(8,128)(2,1)} %get-tuple-element.52), calls=%async_computation.2 | async-start | bytes 3145728 | tf_op jit(solution)/shard_map/all_to_all | solution.py:1149
  231.5 18.8 %collective-permute-done.10.s3_ref = f32[8,8,256]{2,1,0:T(8,128)S(1)} collective-permute-done((f32[8,8,256]{2,1,0:T(8,128)S(1)}, f32[8,8,256]{2,1,0:T(8,128)S(1)}, u32[]{:S(2)}, u32[]{:S(2)}) %collective-permute-start.10) | collective-permute-done | bytes 65568 | tf_op jit(solution)/shard_map/ppermute | solution.py:1154
  252.4 12.4 %gate_back.1 = (f32[2048,384]{1,0:T(8,128)}, bf16[2048,384]{1,0:T(8,128)(2,1)}, bf16[2048,384]{1,0:T(8,128)(2,1)}, bf16[192,256]{1,0:T(8,128)(2,1)}) custom-call(f32[2048,384]{1,0:T(8,128)} %get-tuple-element.53.q_ref, f32[2048,384]{1,0:T(8,128)} %get-tuple-element.50.middle_ref, bf16[8,256,384]{2,1,0:T(8,128)(2,1)} %copy-done.4, ...), custom_call_target="tpu_custom_call" | custom-call | tf_op jit(solution)/shard_map/gate_back/pallas_call | solution.py:751
  265.7 21.0 %conv_back.1 = (f32[16,128,384]{2,1,0:T(8,128)}, bf16[17,256,256]{2,1,0:T(8,128)(2,1)}) custom-call(bf16[16,128,384]{2,1,0:T(8,128)(2,1)} %bitcast.170, bf16[17,256,384]{2,1,0:T(8,128)(2,1)} %get-tuple-element.58.spec_ref, f32[17,256,256]{2,1,0:T(8,128)} %get-tuple-element.48.filter_ref, bf16[8,544,256]{2,1,0:T(8,128)(2,1)} %constant.117.first_ref, ...), custom_call_target="tpu_custom_call" | custom-call | tf_op jit(solution)/shard_map/conv_back/pallas_call | solution.py:817
  286.8 3.5 collective-permute-start.18
  292.1 24.1 %mixer_back.1 = (bf16[8,272,384]{2,1,0:T(8,128)(2,1)}, bf16[192,768]{1,0:T(8,128)(2,1)}, f32[88,384]{1,0:T(8,128)}) custom-call(s32[2]{0:T(128)} %dynamic_slice.83.counts_ref, f32[2048,384]{1,0:T(8,128)} %bitcast.165, bf16[2048,384]{1,0:T(8,128)(2,1)} %get-tuple-element.62.grad_one_ref, ...), custom_call_target="tpu_custom_call" | custom-call | tf_op jit(solution)/shard_map/mixer_back/pallas_call | solution.py:926
  317.2 18.9 %filter_back.1 = (f32[16,128]{1,0:T(8,128)}, f32[128,128]{1,0:T(8,128)}, f32[128,256]{1,0:T(8,128)}, f32[16,128]{1,0:T(8,128)}) custom-call(bf16[17,256,256]{2,1,0:T(8,128)(2,1)} %get-tuple-element.68.cross_ref, bf16[4096,128]{1,0:T(8,128)(2,1)} %get-tuple-element.69.s1_ref, bf16[4096,128]{1,0:T(8,128)(2,1)} %get-tuple-element.70.c1_ref, ...), custom_call_target="tpu_custom_call" | custom-call | tf_op jit(solution)/shard_map/filter_back/pallas_call | solution.py:1027
  342.3 3.5 all-to-all-start.5
  346.0 8.3 %all-to-all-done.5 = bf16[4,496,128]{2,1,0:T(8,128)(2,1)S(1)} async-done(((bf16[4,496,128]{2,1,0:T(8,128)(2,1)}), bf16[4,496,128]{2,1,0:T(8,128)(2,1)S(1)}, u32[]{:S(2)}, u32[]{:S(2)}) %all-to-all-start.5) | async-done | bytes 507936 | tf_op jit(solution)/shard_map/all_to_all | solution.py:1338
  355.1 3.7 collective-permute-start.11
  361.0 4.0 collective-permute-done.11
  370.6 4.3 %all-to-all-start.4 = ((bf16[8,272,384]{2,1,0:T(8,128)(2,1)}), bf16[8,272,384]{2,1,0:T(8,128)(2,1)S(1)}, u32[]{:S(2)}, u32[]{:S(2)}) async-start(bf16[8,272,384]{2,1,0:T(8,128)(2,1)} %get-tuple-element.65), calls=%async_computation.4 | async-start | bytes 3342336 | tf_op jit(solution)/shard_map/all_to_all | solution.py:1149
  392.4 20.1 %all-to-all-done.4.x_ref = bf16[8,272,384]{2,1,0:T(8,128)(2,1)S(1)} async-done(((bf16[8,272,384]{2,1,0:T(8,128)(2,1)}), bf16[8,272,384]{2,1,0:T(8,128)(2,1)S(1)}, u32[]{:S(2)}, u32[]{:S(2)}) %all-to-all-start.4) | async-done | bytes 1671200 | tf_op jit(solution)/shard_map/all_to_all | solution.py:1149
  413.7 4.7 %unpack_grad.1 = f32[4,256,768]{2,1,0:T(8,128)} custom-call(bf16[8,272,384]{2,1,0:T(8,128)(2,1)} %copy-done.6, bf16[4,256,768]{2,1,0:T(8,128)(2,1)} %tokens_ref.1), custom_call_target="tpu_custom_call" | custom-call | tf_op jit(solution)/shard_map/unpack_grad/pallas_call | solution.py:1089
  (281 shorter events, 99.3 us)
Async XLA Ops:
  10.6 46.8 %all-to-all-start = ((bf16[8,272,384]{2,1,0:T(8,128)(2,1)}), bf16[8,272,384]{2,1,0:T(8,128)(2,1)S(1)}, u32[]{:S(2)}, u32[]{:S(2)}) async-start(bf16[8,272,384]{2,1,0:T(8,128)(2,1)} %pack_tokens.1), calls=%async_computation | async-start | bytes 3342336 | tf_op jit(solution)/shard_map/all_to_all | solution.py:1149
  18.1 81.1 %all-gather.3.cloned.1.call-start = ((), (), s32[]{:S(2)}) async-start(), calls=%async_computation.6 | async-start | bytes 1966080 | tf_op jit(solution)/shard_map/all_gather | solution.py:1227
  18.2 27.9 %collective-permute-start.1 = (bf16[32,96]{1,0:T(8,128)(2,1)S(1)}, bf16[32,96]{1,0:T(8,128)(2,1)S(1)}, u32[]{:S(2)}, u32[]{:S(2)}) collective-permute-start(bf16[32,96]{1,0:T(8,128)(2,1)S(1)} %copy-done.33), channel_id=1, source_target_pairs={{1,0},{3,1},{5,2},{7,3},{0,4},{2,5},{4,6},{6,7},{9,8},{11,9},{13,1... | collective-permute-start | bytes 18440 | tf_op jit(solution)/shard_map/ppermute | solution.py:1171
  21.1 25.0 %collective-permute-start = (bf16[32,96]{1,0:T(8,128)(2,1)S(1)}, bf16[32,96]{1,0:T(8,128)(2,1)S(1)}, u32[]{:S(2)}, u32[]{:S(2)}) collective-permute-start(bf16[32,96]{1,0:T(8,128)(2,1)S(1)} %copy-done.33), channel_id=1, source_target_pairs={{0,0},{2,1},{4,2},{6,3},{1,4},{3,5},{5,6},{7,7},{8,8},{10,9},{12,1... | collective-permute-start | bytes 18440 | tf_op jit(solution)/shard_map/ppermute | solution.py:1171
  46.4 3.6 collective-permute-start.4
  46.6 3.9 collective-permute-start.3
  61.2 100.2 %all-to-all-start.1 = ((bf16[8,256,384]{2,1,0:T(8,128)(2,1)}), bf16[8,256,384]{2,1,0:T(8,128)(2,1)S(1)}, u32[]{:S(2)}, u32[]{:S(2)}) async-start(bf16[8,256,384]{2,1,0:T(8,128)(2,1)} %pack_cotangent.1), calls=%async_computation.1 | async-start | bytes 3145728 | tf_op jit(solution)/shard_map/all_to_all | solution.py:1149
  153.5 6.4 %collective-permute-start.7 = (f32[8,8,256]{2,1,0:T(8,128)}, f32[8,8,256]{2,1,0:T(8,128)S(1)}, u32[]{:S(2)}, u32[]{:S(2)}) collective-permute-start(f32[8,8,256]{2,1,0:T(8,128)} %get-tuple-element.51.s0_ref), channel_id=1, source_target_pairs={{0,3},{1,2},{2,1},{3,0},{4,7},{5,6},{6,5},{7,4},{8,11},{9,10},{10,... | collective-permute-start | bytes 196616 | tf_op jit(solution)/shard_map/ppermute | solution.py:1154
  156.4 4.5 %collective-permute-start.6 = (f32[8,8,256]{2,1,0:T(8,128)}, f32[8,8,256]{2,1,0:T(8,128)S(1)}, u32[]{:S(2)}, u32[]{:S(2)}) collective-permute-start(f32[8,8,256]{2,1,0:T(8,128)} %get-tuple-element.51.s0_ref), channel_id=1, source_target_pairs={{0,2},{1,3},{2,0},{3,1},{4,6},{5,7},{6,4},{7,5},{8,10},{9,11},{10,... | collective-permute-start | bytes 196616 | tf_op jit(solution)/shard_map/ppermute | solution.py:1154
  157.0 4.5 %collective-permute-start.5 = (f32[8,8,256]{2,1,0:T(8,128)}, f32[8,8,256]{2,1,0:T(8,128)S(1)}, u32[]{:S(2)}, u32[]{:S(2)}) collective-permute-start(f32[8,8,256]{2,1,0:T(8,128)} %get-tuple-element.51.s0_ref), channel_id=1, source_target_pairs={{0,1},{1,0},{2,3},{3,2},{4,5},{5,4},{6,7},{7,6},{8,9},{9,8},{10,11... | collective-permute-start | bytes 196616 | tf_op jit(solution)/shard_map/ppermute | solution.py:1154
  216.9 74.0 %all-to-all-start.2 = ((bf16[8,256,384]{2,1,0:T(8,128)(2,1)}), bf16[8,256,384]{2,1,0:T(8,128)(2,1)S(1)}, u32[]{:S(2)}, u32[]{:S(2)}) async-start(bf16[8,256,384]{2,1,0:T(8,128)(2,1)} %get-tuple-element.52), calls=%async_computation.2 | async-start | bytes 3145728 | tf_op jit(solution)/shard_map/all_to_all | solution.py:1149
  224.7 25.7 %collective-permute-start.10 = (f32[8,8,256]{2,1,0:T(8,128)S(1)}, f32[8,8,256]{2,1,0:T(8,128)S(1)}, u32[]{:S(2)}, u32[]{:S(2)}) collective-permute-start(f32[8,8,256]{2,1,0:T(8,128)S(1)} %copy-done.20), channel_id=1, source_target_pairs={{0,3},{1,2},{2,1},{3,0},{4,7},{5,6},{6,5},{7,4},{8,11},{9,10},{10,... | collective-permute-start | bytes 196616 | tf_op jit(solution)/shard_map/ppermute | solution.py:1154
  227.6 24.1 %collective-permute-start.9 = (f32[8,8,256]{2,1,0:T(8,128)S(1)}, f32[8,8,256]{2,1,0:T(8,128)S(1)}, u32[]{:S(2)}, u32[]{:S(2)}) collective-permute-start(f32[8,8,256]{2,1,0:T(8,128)S(1)} %copy-done.20), channel_id=1, source_target_pairs={{0,2},{1,3},{2,0},{3,1},{4,6},{5,7},{6,4},{7,5},{8,10},{9,11},{10,... | collective-permute-start | bytes 196616 | tf_op jit(solution)/shard_map/ppermute | solution.py:1154
  228.1 23.6 %collective-permute-start.8 = (f32[8,8,256]{2,1,0:T(8,128)S(1)}, f32[8,8,256]{2,1,0:T(8,128)S(1)}, u32[]{:S(2)}, u32[]{:S(2)}) collective-permute-start(f32[8,8,256]{2,1,0:T(8,128)S(1)} %copy-done.20), channel_id=1, source_target_pairs={{0,1},{1,0},{2,3},{3,2},{4,5},{5,4},{6,7},{7,6},{8,9},{9,8},{10,11... | collective-permute-start | bytes 196616 | tf_op jit(solution)/shard_map/ppermute | solution.py:1154
  228.5 58.2 %collective-permute-start.15 = (bf16[480,256]{1,0:T(8,128)(2,1)S(1)}, bf16[480,256]{1,0:T(8,128)(2,1)S(1)}, u32[]{:S(2)}, u32[]{:S(2)}) collective-permute-start(bf16[480,256]{1,0:T(8,128)(2,1)S(1)} %reduce_sum.94), channel_id=1, source_target_pairs={{0,4},{1,5},{2,6},{3,7},{4,0},{5,1},{6,2},{7,3},{8,12},{9,13},{10,... | collective-permute-start | bytes 737288 | tf_op jit(solution)/shard_map/ppermute | solution.py:1310
  286.8 59.0 %collective-permute-start.18 = (bf16[480,256]{1,0:T(8,128)(2,1)S(1)}, bf16[480,256]{1,0:T(8,128)(2,1)S(1)}, u32[]{:S(2)}, u32[]{:S(2)}) collective-permute-start(bf16[480,256]{1,0:T(8,128)(2,1)S(1)} %add_convert_fusion), channel_id=1, source_target_pairs={{0,3},{1,2},{2,1},{3,0},{4,7},{5,6},{6,5},{7,4},{8,11},{9,10},{10,... | collective-permute-start | bytes 737288 | tf_op jit(solution)/shard_map/ppermute | solution.py:1154
  290.3 55.5 %collective-permute-start.17 = (bf16[480,256]{1,0:T(8,128)(2,1)S(1)}, bf16[480,256]{1,0:T(8,128)(2,1)S(1)}, u32[]{:S(2)}, u32[]{:S(2)}) collective-permute-start(bf16[480,256]{1,0:T(8,128)(2,1)S(1)} %add_convert_fusion), channel_id=1, source_target_pairs={{0,2},{1,3},{2,0},{3,1},{4,6},{5,7},{6,4},{7,5},{8,10},{9,11},{10,... | collective-permute-start | bytes 737288 | tf_op jit(solution)/shard_map/ppermute | solution.py:1154
  290.3 55.5 %collective-permute-start.16 = (bf16[480,256]{1,0:T(8,128)(2,1)S(1)}, bf16[480,256]{1,0:T(8,128)(2,1)S(1)}, u32[]{:S(2)}, u32[]{:S(2)}) collective-permute-start(bf16[480,256]{1,0:T(8,128)(2,1)S(1)} %add_convert_fusion), channel_id=1, source_target_pairs={{0,1},{1,0},{2,3},{3,2},{4,5},{5,4},{6,7},{7,6},{8,9},{9,8},{10,11... | collective-permute-start | bytes 737288 | tf_op jit(solution)/shard_map/ppermute | solution.py:1154
  342.3 12.1 %all-to-all-start.5 = ((bf16[4,496,128]{2,1,0:T(8,128)(2,1)}), bf16[4,496,128]{2,1,0:T(8,128)(2,1)S(1)}, u32[]{:S(2)}, u32[]{:S(2)}) async-start(bf16[4,496,128]{2,1,0:T(8,128)(2,1)} %bitcast.122), calls=%async_computation.5 | async-start | bytes 1015808 | tf_op jit(solution)/shard_map/all_to_all | solution.py:1338
  355.1 9.9 %collective-permute-start.11 = (bf16[496,128]{1,0:T(8,128)(2,1)}, bf16[496,128]{1,0:T(8,128)(2,1)}, u32[]{:S(2)}, u32[]{:S(2)}) collective-permute-start(bf16[496,128]{1,0:T(8,128)(2,1)} %reduce_sum.87), channel_id=1, source_target_pairs={{0,4},{1,5},{2,6},{3,7},{4,0},{5,1},{6,2},{7,3},{8,12},{9,13},{10,... | collective-permute-start | bytes 380936 | tf_op jit(solution)/shard_map/ppermute | solution.py:1310
  366.1 11.3 %collective-permute-start.14 = (bf16[496,128]{1,0:T(8,128)(2,1)S(1)}, bf16[496,128]{1,0:T(8,128)(2,1)S(1)}, u32[]{:S(2)}, u32[]{:S(2)}) collective-permute-start(bf16[496,128]{1,0:T(8,128)(2,1)S(1)} %add_convert_fusion.1), channel_id=1, source_target_pairs={{0,3},{1,2},{2,1},{3,0},{4,7},{5,6},{6,5},{7,4},{8,11},{9,10},{10,... | collective-permute-start | bytes 380936 | tf_op jit(solution)/shard_map/ppermute | solution.py:1154
  366.3 11.1 %collective-permute-start.13 = (bf16[496,128]{1,0:T(8,128)(2,1)S(1)}, bf16[496,128]{1,0:T(8,128)(2,1)S(1)}, u32[]{:S(2)}, u32[]{:S(2)}) collective-permute-start(bf16[496,128]{1,0:T(8,128)(2,1)S(1)} %add_convert_fusion.1), channel_id=1, source_target_pairs={{0,2},{1,3},{2,0},{3,1},{4,6},{5,7},{6,4},{7,5},{8,10},{9,11},{10,... | collective-permute-start | bytes 380936 | tf_op jit(solution)/shard_map/ppermute | solution.py:1154
  369.0 8.3 %collective-permute-start.12 = (bf16[496,128]{1,0:T(8,128)(2,1)S(1)}, bf16[496,128]{1,0:T(8,128)(2,1)S(1)}, u32[]{:S(2)}, u32[]{:S(2)}) collective-permute-start(bf16[496,128]{1,0:T(8,128)(2,1)S(1)} %add_convert_fusion.1), channel_id=1, source_target_pairs={{0,1},{1,0},{2,3},{3,2},{4,5},{5,4},{6,7},{7,6},{8,9},{9,8},{10,11... | collective-permute-start | bytes 380936 | tf_op jit(solution)/shard_map/ppermute | solution.py:1154
  370.6 42.0 %all-to-all-start.4 = ((bf16[8,272,384]{2,1,0:T(8,128)(2,1)}), bf16[8,272,384]{2,1,0:T(8,128)(2,1)S(1)}, u32[]{:S(2)}, u32[]{:S(2)}) async-start(bf16[8,272,384]{2,1,0:T(8,128)(2,1)} %get-tuple-element.65), calls=%async_computation.4 | async-start | bytes 3342336 | tf_op jit(solution)/shard_map/all_to_all | solution.py:1149
  (38 other events, 343.5 us)
Sparse Core Ops, SparseCore 0:
  25.5 21.4 all-gather.2
